TPU v7x, 128 devices: a whole 4x4x4 slice. The times are simulated.
128 devices in a mesh: seq: 4 (over z), head: 32 (over y, x, core).
Axes of the slice: x: 4, y: 4, z: 4, core: 2. Of those that a mesh axis runs over, the one named last changes fastest.
Arguments:
- queries: float32 [8192, 4096], P('seq', 'head'), may hold values from -6 to 6
- key_rows: float32 [8192, 4096], P('seq', 'head'), may hold values from -6 to 6
- values: float32 [8192, 4096], P('seq', 'head'), may hold values from -6 to 6
- out_weight: bfloat16 [4096, 2048], P('head'), may hold values from -0.09375 to 0.09375
- expert_ids: int32 [8192, 8], P(('seq', 'head')), may hold values from 0 to 127, all different within a row; in each aligned block of 64 rows (0 to 63, 64 to 127, ...) at most 8 rows name the same one
- gate_ints: int32 [8192, 8], P(('seq', 'head')), may hold values from 1 to 1023
- w_gate: bfloat16 [128, 2048, 768], P(('seq', 'head')), may hold values from -0.125 to 0.125
- w_up: bfloat16 [128, 2048, 768], P(('seq', 'head')), may hold values from -0.125 to 0.125
- w_down: bfloat16 [128, 768, 2048], P(('seq', 'head')), may hold values from -0.21875 to 0.21875
Outputs:
- layer_out: float32 [8192, 2048], P(('seq', 'head'))
Inputs may be any that keep to these rules, and one draw needn't show every extreme that they name: `expert_ids`: each row names 8 different experts. Within the rows of one device (aligned blocks of 64 rows) no expert is named more than 8 times, a bound that some block reaches.
All inputs are finite; a program needn't handle non-finite values.
Results may differ from a plain program's by a relative error of at most 0.017.
Values may be sent and summed in bfloat16 or wider, within the bound.
A program may use at most 128 MiB of HBM per device.

v0:
```python
import math

import jax
import jax.numpy as jnp
from jax import lax
from jax.sharding import PartitionSpec as P

DH = 128


HIGH = lax.Precision.HIGHEST


def cut_along(array, dim, devices):
    dims = array.shape
    blocks = array.reshape(*dims[:dim], devices, dims[dim] // devices, *dims[dim + 1 :])
    return jnp.moveaxis(blocks, dim, 0)


def laid_out(blocks, dim):
    blocks = jnp.moveaxis(blocks, 0, dim)
    dims = blocks.shape
    return blocks.reshape(*dims[:dim], dims[dim] * dims[dim + 1], *dims[dim + 2 :])


def exchange_both(array, axis, axes, splits, concats):
    sizes = [lax.axis_size(a) for a in axes]
    blocks = cut_along(array, splits[0], sizes[0])
    blocks = jnp.moveaxis(cut_along(blocks, splits[1] + 1, sizes[1]), 0, 1)
    inside = blocks.shape[2:]
    blocks = blocks.reshape(-1, *inside)
    blocks = lax.all_to_all(blocks, axis, split_axis=0, concat_axis=0, tiled=True)
    blocks = laid_out(blocks.reshape(*sizes, *inside), concats[0] + 1)
    return laid_out(blocks, concats[1])


def causal_linear(query_heads, key_heads, value_heads):
    heads, length, width = query_heads.shape
    block = math.gcd(512, length)
    count = length // block

    def split(array):
        return array.reshape(heads, count, block, width).transpose(1, 0, 2, 3)

    lower = jnp.tril(jnp.ones((block, block), jnp.float32))

    def advance(state, inputs):
        query_block, key_block, value_block = inputs
        scores = jnp.einsum("hid,hjd->hij", query_block, key_block, precision=HIGH) * lower
        output = jnp.einsum("hij,hjd->hid", scores, value_block, precision=HIGH)
        output = output + jnp.einsum("hid,hde->hie", query_block, state, precision=HIGH)
        state = state + jnp.einsum("hjd,hje->hde", key_block, value_block, precision=HIGH)
        return (state, output)

    start = jnp.zeros((heads, width, width), jnp.float32)
    state, outputs = lax.scan(
        advance, start, (split(query_heads), split(key_heads), split(value_heads))
    )
    return (outputs.transpose(1, 0, 2, 3).reshape(heads, length, width), state)


def shards(queries, key_rows, values, out_weight, expert_ids, gate_ints, w_gate, w_up, w_down):
    length = queries.shape[0]
    heads_here = queries.shape[1] // DH

    def split_heads(array):
        return array.reshape(length, heads_here, DH).transpose(1, 0, 2)

    query_heads = split_heads(queries)
    local_out, local_state = causal_linear(query_heads, split_heads(key_rows), split_heads(values))
    every_state = lax.all_gather(
        local_state[None].astype(jnp.bfloat16), "seq", axis=0, tiled=True
    ).astype(jnp.float32)
    before = (jnp.arange(every_state.shape[0], dtype=jnp.int32) < lax.axis_index("seq")).astype(
        jnp.float32
    )
    earlier = jnp.sum(every_state * before[:, None, None, None], axis=0)
    heads_out = local_out + jnp.einsum("hid,hde->hie", query_heads, earlier, precision=HIGH)
    heads_out = heads_out * lax.rsqrt(
        jnp.mean(heads_out * heads_out, axis=-1, keepdims=True) + 1e-06
    )
    attn = heads_out.transpose(1, 0, 2).reshape(length, heads_here * DH).astype(jnp.bfloat16)
    head_count = lax.axis_size("head")
    seq_count = lax.axis_size("seq")
    tok_count = length // head_count
    all_heads = lax.all_to_all(attn, "head", split_axis=0, concat_axis=1, tiled=True)
    all_rows = lax.all_gather(out_weight, "head", axis=0, tiled=True)
    projected = jnp.dot(all_heads, all_rows, preferred_element_type=jnp.float32)
    normed = (
        projected * lax.rsqrt(jnp.mean(projected * projected, axis=-1, keepdims=True) + 1e-06)
    ).astype(jnp.bfloat16)
    gates = gate_ints.astype(jnp.float32)
    gates = gates / jnp.sum(gates, axis=-1, keepdims=True)
    top_count = expert_ids.shape[1]
    local_experts = w_gate.shape[0]
    devices = seq_count * head_count
    experts = local_experts * devices
    capacity = max(2, 2 * tok_count * top_count // experts)
    width = normed.shape[1]
    flat_ids = expert_ids.reshape(-1)
    assigned = flat_ids.shape[0]
    onehot = (flat_ids[:, None] == jnp.arange(experts, dtype=jnp.int32)[None, :]).astype(jnp.int32)
    before_count = jnp.cumsum(onehot, axis=0, dtype=jnp.int32) - onehot
    position = jnp.sum(before_count * onehot, axis=1, dtype=jnp.int32)
    slot_index = flat_ids * capacity + position
    source = (
        jnp.zeros((experts * capacity,), jnp.int32)
        .at[slot_index]
        .set(jnp.arange(assigned, dtype=jnp.int32))
    )
    filled = jnp.zeros((experts * capacity,), jnp.bool_).at[slot_index].set(True)
    picked = normed[source // top_count]
    outgoing = jnp.where(filled[:, None], picked, jnp.zeros_like(picked))
    outgoing = outgoing.reshape(seq_count, head_count, local_experts, capacity, width)
    received = exchange_both(outgoing, ("seq", "head"), ("seq", "head"), (0, 1), (0, 1))
    expert_received = received.reshape(devices, local_experts, capacity, width)
    gate_val = jnp.einsum(
        "nesd,edf->nesf", expert_received, w_gate, preferred_element_type=jnp.float32
    )
    up_val = jnp.einsum("nesd,edf->nesf", expert_received, w_up, preferred_element_type=jnp.float32)
    act = (jax.nn.silu(gate_val) * up_val).astype(jnp.bfloat16)
    result = jnp.einsum("nesf,efd->nesd", act, w_down, preferred_element_type=jnp.float32).astype(
        jnp.bfloat16
    )
    result = result.reshape(seq_count, head_count, local_experts, capacity, width)
    returned = exchange_both(result, ("seq", "head"), ("seq", "head"), (0, 1), (0, 1))
    returned = returned.reshape(experts * capacity, width)
    gathered = returned[slot_index].astype(jnp.float32) * gates.reshape(-1)[:, None]
    mixture = jnp.sum(gathered.reshape(tok_count, top_count, width), axis=1)
    return projected + mixture


def solution(mesh):
    placed = (
        P("seq", "head"),
        P("seq", "head"),
        P("seq", "head"),
        P("head", None),
        P(("seq", "head"), None),
        P(("seq", "head"), None),
        P(("seq", "head"), None, None),
        P(("seq", "head"), None, None),
        P(("seq", "head"), None, None),
    )
    return jax.shard_map(
        shards, mesh=mesh, in_specs=placed, out_specs=P(("seq", "head"), None), check_vma=False
    )
```

profile of v0, /device:TPU:3, one launch (start us, length us, event | category | flops | bytes accessed | tf_op | source)
XLA Modules:
  0.0 275.0 jit_solution(5523111241887061232)
XLA Ops:
  6.5 0.0 copy-start
  6.5 0.0 all-gather.3.cloned.1.call-start
  6.5 0.7 all-gather.3.cloned.1.call-update
  7.3 30.9 %while.13 = (s32[]{:T(128)}, f32[1,128,128]{2,1,0:T(8,128)S(1)}, f32[4,1,512,128]{3,2,1,0:T(8,128)}, f32[4,1,512,128]{3,2,1,0:T(8,128)}, f32[4,1,512,128]{3,2,1,...) while((s32[]{:T(128)}, f32[1,128,128]{2,1,0:T(8,128)S(1)}, ...), condition=%wide.region_1.2_spmd.clone, body=%wide.region_0.1_spmd.clone.sunk | while | flops 1007534080 | bytes 4656736 | solution.py:56
  7.3 2.2 convolution_multiply_fusion.2
  9.5 1.9 fusion.89
  11.5 2.0 fusion.90
  13.5 1.6 fusion.88
  15.1 2.0 convolution_multiply_fusion.2
  17.2 1.9 fusion.89
  19.1 2.0 fusion.90
  21.1 1.7 fusion.88
  22.8 2.0 convolution_multiply_fusion.2
  24.9 1.9 fusion.89
  26.8 2.0 fusion.90
  28.8 1.7 fusion.88
  30.5 2.0 convolution_multiply_fusion.2
  32.5 1.9 fusion.89
  34.5 2.0 fusion.90
  36.5 1.6 fusion.88
  38.2 2.6 copy.37
  40.8 11.2 %all-gather = bf16[4,128,128]{2,1,0:T(8,128)(2,1)S(1)} all-gather(bf16[1,128,128]{2,1,0:T(8,128)(2,1)S(1)} %convert_element_type.66), channel_id=2, replica_groups=mesh['seq'=4,'head'=32] {'seq'}, dimensions={0}, use_global_device_ids=true | all-gather | bytes 163840 | tf_op jit(solution)/shard_map/all_gather | solution.py:71
  51.9 0.1 fusion.50
  52.0 0.0 copy-start.3
  52.0 2.7 multiply_reduce_fusion
  54.8 0.9 multiply_convert_fusion
  55.7 2.1 copy.26
  57.8 9.9 %all-to-all-start = ((bf16[32,64,128]{2,1,0:T(8,128)(2,1)}), bf16[32,64,128]{2,1,0:T(8,128)(2,1)}, u32[]{:S(2)}, u32[]{:S(2)}) async-start(bf16[32,64,128]{2,1,0:T(8,128)(2,1)} %bitcast.182), calls=%async_computation | async-start | bytes 1048576 | tf_op jit(solution)/shard_map/all_to_all | solution.py:86
  67.7 0.0 copy-done.3
  67.7 0.1 copy.29
  67.8 0.1 eq.29
  67.9 0.1 eq.25
  67.9 0.1 copy.31
  68.1 0.2 fusion.51
  68.4 0.2 fusion.49
  68.6 0.1 copy.28
  68.7 0.1 mul.78
  68.8 2.4 scatter_custom_fusion.1
  71.3 2.6 scatter_custom_fusion
  73.9 0.1 broadcast_in_dim.56
  74.0 10.0 %all-to-all-done = bf16[32,64,128]{2,1,0:T(8,128)(2,1)} async-done(((bf16[32,64,128]{2,1,0:T(8,128)(2,1)}), bf16[32,64,128]{2,1,0:T(8,128)(2,1)}, u32[]{:S(2)}, u32[]{:S(2)}) %all-to-all-start) | async-done | bytes 524320 | tf_op jit(solution)/shard_map/all_to_all | solution.py:86
  84.0 6.4 %all-gather.3.cloned.1.call-done = bf16[4096,2048]{1,0:T(8,128)(2,1)} async-done(((bf16[128,2048]{1,0:T(8,128)(2,1)}), bf16[4096,2048]{1,0:T(8,128)(2,1)}) %all-gather.3.cloned.1.call-update) | async-done | bytes 16777232 | tf_op jit(solution)/shard_map/all_gather | solution.py:87
  90.4 9.1 %multiply_reduce_fusion.1 = (f32[64]{0:T(128)S(1)}, f32[64,2048]{1,0:T(8,128)S(1)}) fusion(bf16[4096,2048]{1,0:T(8,128)(2,1)} %all-gather.3.cloned.1.call-done, bf16[32,64,128]{2,1,0:T(8,128)(2,1)} %all-to-all-done), kind=kOutput, calls=%fused_computation.59 | convolution fusion | flops 1074003968 | bytes 17826048 | tf_op jit(solution)/shard_map/dot_general | solution.py:88
  99.5 0.0 copy-start.1
  99.5 0.8 copy-done.1
  100.3 0.1 multiply_convert_fusion.1
  100.4 6.0 %gather_fusion = bf16[1024,2048]{1,0:T(8,128)(2,1)} fusion(bf16[64,2048]{1,0:T(8,128)(2,1)S(1)} %multiply_convert_fusion.1, s32[1024]{0:T(1024)S(1)} %fusion.55), kind=kCustom, calls=%fused_computation | custom fusion | bytes 8392704 | tf_op jit(solution)/shard_map/gather | solution.py:112
  106.4 2.5 bitcast_select_fusion
  109.0 59.2 %all_to_all.26 = bf16[128,1,1,1,8,2048]{5,4,3,2,1,0:T(8,128)(2,1)S(1)} all-to-all(bf16[128,1,1,1,8,2048]{5,4,3,2,1,0:T(8,128)(2,1)S(1)} %bitcast_select_fusion), channel_id=1, replica_groups=mesh['seq'=4,'head'=32] {'seq','head'}, dimensions={0} | all-to-all | bytes 8388608 | tf_op jit(solution)/shard_map/all_to_all | solution.py:32
  168.1 2.3 copy.34
  170.4 0.0 copy-start.2
  170.4 2.0 copy-done.2
  172.4 0.0 copy-done.5
  172.4 5.2 %fusion.30 = f32[128,8,768]{2,0,1:T(8,128)} fusion(bf16[128,8,2048]{2,0,1:T(8,128)(2,1)S(1)} %bitcast.180, bf16[1,2048,768]{2,1,0:T(8,128)(2,1)S(1)} %copy-done.5), kind=kOutput, calls=%fused_computation.41 | convolution fusion | flops 3221225472 | bytes 10485760 | tf_op jit(solution)/shard_map/nesd,edf->nesf/dot_general | solution.py:120
  177.6 0.0 copy-done
  177.6 12.3 %convert_bitcast_fusion = bf16[128,1,1,1,8,2048]{5,0,4,3,2,1:T(8,128)(2,1)} fusion(bf16[1,768,2048]{2,1,0:T(8,128)(2,1)S(1)} %copy-done, f32[128,8,768]{2,0,1:T(8,128)} %fusion.30, bf16[128,8,2048]{2,0,1:T(8,128)(2,1)} %bitcast.181, bf16[1,2048,768]{2,1,0:T(8,128)(2,1)} %param.17), kind=kOutput, calls=%fused_computation.37 | convolution fusion | flops 6449266688 | bytes 17825792 | tf_op jit(solution)/shard_map/nesf,efd->nesd/dot_general | solution.py:122
  189.9 6.5 %copy.35 = bf16[128,1,1,1,8,2048]{5,4,3,2,1,0:T(8,128)(2,1)} copy(bf16[128,1,1,1,8,2048]{5,0,4,3,2,1:T(8,128)(2,1)} %convert_bitcast_fusion) | data formatting | bytes 8388608 | tf_op jit(solution)/shard_map/reshape;transpose;transpose;reshape;reshape;reshape | solution.py:31
  196.4 6.9 %all-to-all-start.2 = ((bf16[128,1,1,1,8,2048]{5,4,3,2,1,0:T(8,128)(2,1)}), bf16[128,1,1,1,8,2048]{5,4,3,2,1,0:T(8,128)(2,1)}, u32[]{:S(2)}, u32[]{:S(2)}) async-start(bf16[128,1,1,1,8,2048]{5,4,3,2,1,0:T(8,128)(2,1)} %copy.35), calls=%async_computation.2 | async-start | bytes 8388608 | tf_op jit(solution)/shard_map/all_to_all | solution.py:32
  203.2 0.0 copy-done.4
  203.3 0.1 copy.36
  203.4 51.4 %all-to-all-done.2 = bf16[128,1,1,1,8,2048]{5,4,3,2,1,0:T(8,128)(2,1)} async-done(((bf16[128,1,1,1,8,2048]{5,4,3,2,1,0:T(8,128)(2,1)}), bf16[128,1,1,1,8,2048]{5,4,3,2,1,0:T(8,128)(2,1)}, u32[]{:S(2)}, u32[]{:S(2)}) %all-to-all-start.2) | async-done | bytes 4194336 | tf_op jit(solution)/shard_map/all_to_all | solution.py:32
  254.8 8.0 %gather_fusion.1 = bf16[512,2048]{1,0:T(8,128)(2,1)} fusion(bf16[1024,2048]{1,0:T(8,128)(2,1)} %bitcast.46, s32[1024]{0:T(1024)S(1)} %pad_clamp_fusion), kind=kCustom, calls=%fused_computation.1 | custom fusion | bytes 4196352 | tf_op jit(solution)/shard_map/gather | solution.py:128
  262.8 3.4 %fusion.27 = f32[64,2048]{1,0:T(8,128)S(1)} fusion(bf16[512,2048]{1,0:T(8,128)(2,1)} %gather_fusion.1, f32[64,8]{1,0:T(8,128)S(1)} %copy.36), kind=kLoop, calls=%fused_computation.35 | loop fusion | flops 3014656 | bytes 2623488 | tf_op jit(solution)/shard_map/reduce_sum | solution.py:129
  266.2 1.9 add.82
  (22 shorter events, 0.2 us)
Async XLA Ops:
  6.5 171.1 %copy-start = (bf16[1,768,2048]{2,1,0:T(8,128)(2,1)S(1)}, bf16[1,768,2048]{2,1,0:T(8,128)(2,1)}, u32[]{:S(2)}) copy-start(bf16[1,768,2048]{2,1,0:T(8,128)(2,1)} %param.19) | copy-start | bytes 9437188
  6.5 83.9 %all-gather.3.cloned.1.call-start = ((), (), s32[]{:S(2)}) async-start(), calls=%async_computation.3 | async-start | bytes 17301504 | tf_op jit(solution)/shard_map/all_gather | solution.py:87
  52.0 15.6 %copy-start.3 = (s32[64,8]{0,1:T(8,128)S(1)}, s32[64,8]{0,1:T(8,128)}, u32[]{:S(2)}) copy-start(s32[64,8]{0,1:T(8,128)} %param.15) | copy-start | bytes 6148
  57.8 26.3 %all-to-all-start = ((bf16[32,64,128]{2,1,0:T(8,128)(2,1)}), bf16[32,64,128]{2,1,0:T(8,128)(2,1)}, u32[]{:S(2)}, u32[]{:S(2)}) async-start(bf16[32,64,128]{2,1,0:T(8,128)(2,1)} %bitcast.182), calls=%async_computation | async-start | bytes 1048576 | tf_op jit(solution)/shard_map/all_to_all | solution.py:86
  99.5 0.8 copy-start.1
  168.1 4.3 %copy-start.5 = (bf16[1,2048,768]{2,1,0:T(8,128)(2,1)S(1)}, bf16[1,2048,768]{2,1,0:T(8,128)(2,1)}, u32[]{:S(2)}) copy-start(bf16[1,2048,768]{2,1,0:T(8,128)(2,1)} %param.18) | copy-start | bytes 9437188
  170.4 2.0 copy-start.2
  196.4 6.9 %copy-start.4 = (s32[64,8]{0,1:T(8,128)S(1)}, s32[64,8]{0,1:T(8,128)}, u32[]{:S(2)}) copy-start(s32[64,8]{0,1:T(8,128)} %param.16) | copy-start | bytes 6148
  196.4 58.4 %all-to-all-start.2 = ((bf16[128,1,1,1,8,2048]{5,4,3,2,1,0:T(8,128)(2,1)}), bf16[128,1,1,1,8,2048]{5,4,3,2,1,0:T(8,128)(2,1)}, u32[]{:S(2)}, u32[]{:S(2)}) async-start(bf16[128,1,1,1,8,2048]{5,4,3,2,1,0:T(8,128)(2,1)} %copy.35), calls=%async_computation.2 | async-start | bytes 8388608 | tf_op jit(solution)/shard_map/all_to_all | solution.py:32
Sparse Core Ops, SparseCore 0:
  9.6 80.7 all-gather.2
where the time goes:
time: 278 us; the launch traced here: 275 us
  blocking collectives  70.3 us (25%)
  waiting for transfers between devices  68.5 us (25%)
  matrix products  60 us (22%)
  local copies, waits for them, and re-layouts  36.1 us (13%)
  starting transfers between devices  16.8 us (6%)
  between operations  13.6 us (5%)
  other arithmetic  9.54 us (3%)
    all_to_all x1, blocking collectives, exchange_both(): lax.all_to_all(blocks, axis, split_axis=0, concat_axis=0, tiled=True)  59.2 us
    all_to_all x1, waiting for transfers between devices, exchange_both(): lax.all_to_all(blocks, axis, split_axis=0, concat_axis=0, tiled=True)  51.4 us
    dot_general x1, matrix products, shards(): jnp.einsum('nesf,efd->nesd', act, w_down, preferred_element_type=jnp.floa...  12.3 us
    all_gather x1, blocking collectives, shards(): lax.all_gather(local_state[None].astype(jnp.bfloat16), 'seq', axis=0, til...  11.2 us
    all_to_all x1, waiting for transfers between devices, shards(): lax.all_to_all(attn, 'head', split_axis=0, concat_axis=1, tiled=True)  9.98 us
    all_to_all x1, starting transfers between devices, shards(): lax.all_to_all(attn, 'head', split_axis=0, concat_axis=1, tiled=True)  9.89 us
    dot_general x1, matrix products, shards(): projected = jnp.dot(all_heads, all_rows, preferred_element_type=jnp.float32)  9.08 us
    dot_general x4, matrix products, advance(): jnp.einsum('hid,hjd->hij', query_block, key_block, precision=HIGH) * lower  8.27 us
  transfers between devices with their start and end apart: 3, of which 3 were waited for; matrix products, arithmetic and copies ran while one was open for 17% of the time, Pallas kernels for 0%

commit v1 on v0

v1 whole, which is shorter than its diff:
```python
import functools

import jax
import jax.numpy as jnp
from jax import lax
from jax.experimental import pallas as pl
from jax.experimental.pallas import tpu as pltpu
from jax.sharding import PartitionSpec as P

MESH = pl.DeviceIdType.MESH
BF = jnp.bfloat16
F32 = jnp.float32
COLS = (768, 640, 640)
OFF = (0, 768, 1408)
PLANE = ((1, 2), (0, 2), (0, 1))
ORDER = (5, 10, 2, 8, 15, 7, 13, 1, 4, 11, 14, 3, 12, 6, 9)
CB = 4
CBW = 512
CHUNK = 256


def partners():
    found = []
    for a in range(4):
        for b in range(4):
            for d in range(4):
                if 0 in (a, b, d) and (a, b, d) != (0, 0, 0):
                    found.append((a, b, d, 0))
    found.append((0, 0, 0, 1))
    for a in range(1, 4):
        found += [(a, 0, 0, 1), (0, a, 0, 1), (0, 0, a, 1)]
    return found


def body(
    q_h, k_h, v_h, w_h, ids_ref, gi_ref, wg_h, wu_h, wd_h, out_ref,
    q_s, k_s, v_s, o_s, st_s, st_r, at_s, at_r, w_s, rs_s, rs_r, pf_s, pj_s,
    vg_s, m0, m1, m2, sel_s, com_s, l0, l1, l2, ds0, ds1, ds2, r0, r1, r2,
    o0, o1, o2, rt0, rt1, rt2, ps0, ps1, ps2, pr0, pr1, pr2, wg_s, wu_s, wd_s,
    loc_sem, st_ss, st_rs, at_ss, at_rs, w_ss, w_rs, wf_ss, wf_rs, rs_ss, rs_rs,
    m_ss, m_rs, l_ss, l_rs, d_ss, d_rs, e_ss, e_rs, p_ss, p_rs,
):
    meta, line = (m0, m1, m2), (l0, l1, l2)
    ds, rr, oo, rt = (ds0, ds1, ds2), (r0, r1, r2), (o0, o1, o2), (rt0, rt1, rt2)
    ps, pr = (ps0, ps1, ps2), (pr0, pr1, pr2)
    z = lax.axis_index("seq")
    head = lax.axis_index("head")
    y, x, c = head // 8, (head // 2) % 4, head % 2
    at = (x, y, z)
    other = 1 - c

    def dev(coords, core):
        return (coords[2], (coords[1] * 4 + coords[0]) * 2 + core)

    def moved(**shift):
        return tuple((at[i] + shift.get("xyz"[i], 0)) % 4 for i in range(3))

    def along(axis, d):
        return tuple((at[i] + d) % 4 if i == axis else at[i] for i in range(3))

    sent = []

    def send(src, dst, ss, rs, device):
        copy = pltpu.make_async_remote_copy(
            src_ref=src, dst_ref=dst, send_sem=ss, recv_sem=rs, device_id=device, device_id_type=MESH
        )
        copy.start()
        sent.append(copy)
        return copy

    loads = []
    for i, (src, dst) in enumerate(
        ((k_h, k_s), (v_h, v_s), (q_h, q_s), (w_h, w_s.at[y, c]), (wg_h, wg_s), (wu_h, wu_s), (wd_h, wd_s))
    ):
        copy = pltpu.make_async_copy(src, dst, loc_sem.at[i])
        copy.start()
        loads.append(copy)

    barrier = pltpu.get_barrier_semaphore()
    greeted = partners()
    for dx, dy, dz, dc in greeted:
        core = other if dc else c
        pl.semaphore_signal(
            barrier, inc=1, device_id=dev(moved(x=dx, y=dy, z=dz), core), device_id_type=MESH
        )

    experts = lax.broadcasted_iota(jnp.int32, (64, 128), 1)
    named = jnp.zeros((64, 128), F32)
    gate = jnp.zeros((64, 128), F32)
    gates = gi_ref[...].astype(F32)
    gates = gates / jnp.sum(gates, axis=-1, keepdims=True)
    for k in range(8):
        hit = ids_ref[:, k : k + 1] == experts
        named = jnp.where(hit, 1.0, named)
        gate = jnp.where(hit, gates[:, k : k + 1], gate)
    before = (
        lax.broadcasted_iota(jnp.int32, (64, 64), 1) < lax.broadcasted_iota(jnp.int32, (64, 64), 0)
    ).astype(F32).astype(BF)
    rank = jnp.dot(before, named.astype(BF), preferred_element_type=F32)
    vg_s[:, :128] = jnp.where(named > 0.5, rank, -1.0).astype(BF)
    vg_s[:, 128:] = gate.astype(BF)

    pl.semaphore_wait(barrier, len(greeted))

    meta_in = []
    for p in range(3):
        meta[p][at[p], c] = vg_s[...]
        for i in range(1, 8):
            d, k = i // 2, i % 2
            meta_in.append(
                send(
                    vg_s, meta[p].at[at[p], c], m_ss.at[p * 8 + i], m_rs.at[p * 8 + i],
                    dev(along(p, d), other if k else c),
                )
            )
    loads[3].wait()
    mine = w_s.at[y, c]
    w_in = [send(mine, mine, w_ss.at[d], w_rs.at[d], dev(along(1, d), c)) for d in (2, 1, 3)]
    wf_in = [send(mine, mine, wf_ss.at[0], wf_rs.at[0], dev(at, other))]

    loads[0].wait()
    loads[1].wait()
    count = q_s.shape[0]
    state = jnp.zeros((128, 128), F32)
    prefix = []
    for i in range(count):
        prefix.append(state)
        state = state + lax.dot_general(
            k_s[i].astype(BF), v_s[i].astype(BF), (((0,), (0,)), ((), ())), preferred_element_type=F32
        )
    st_s[...] = state.astype(BF)
    st_in = [
        send(st_s, st_r.at[z], st_ss.at[d], st_rs.at[d], dev(along(2, d), c)) for d in (1, 2, 3)
    ]
    loads[2].wait()
    lower = lax.broadcasted_iota(jnp.int32, (CHUNK, CHUNK), 1) <= lax.broadcasted_iota(
        jnp.int32, (CHUNK, CHUNK), 0
    )
    for i in range(count):
        qb, kb = q_s[i].astype(BF), k_s[i].astype(BF)
        scores = lax.dot_general(qb, kb, (((1,), (1,)), ((), ())), preferred_element_type=F32)
        scores = jnp.where(lower, scores, 0.0).astype(BF)
        o_s[i] = jnp.dot(scores, v_s[i].astype(BF), preferred_element_type=F32)
    for copy in st_in:
        copy.wait_recv()
    earlier = jnp.zeros((128, 128), F32)
    for d in (1, 2, 3):
        source = (z - d + 4) % 4
        earlier = earlier + jnp.where(source < z, st_r[source].astype(F32), 0.0)
    for i in range(count):
        total = (prefix[i] + earlier).astype(BF)
        mixed = o_s[i] + jnp.dot(q_s[i].astype(BF), total, preferred_element_type=F32)
        mixed = mixed * lax.rsqrt(jnp.mean(mixed * mixed, axis=-1, keepdims=True) + 1e-06)
        mixed = mixed.astype(BF)
        for j in range(2):
            for k in range(2):
                at_s[i // 2, k, (i % 2) * 2 + j] = mixed[(2 * j + k) * 64 : (2 * j + k + 1) * 64]
    at_in = []
    for i in (4, 5, 2, 3, 6, 7, 1):
        d, k = i // 2, i % 2
        to = (y + d) % 4
        core = other if k else c
        at_in.append(
            send(at_s.at[to, core], at_r.at[y, c], at_ss.at[i], at_rs.at[i], dev(along(1, d), core))
        )
    at_r[y, c] = at_s[y, c]

    for copy in meta_in:
        copy.wait_recv()
    row_e = lax.broadcasted_iota(jnp.int32, (128, 256), 0)
    col_r = lax.broadcasted_iota(jnp.int32, (128, 256), 1)
    first, second = col_r // 64, (col_r // 16) % 4
    same = (row_e // 64) == ((col_r // 8) % 2)
    slot = jnp.where(same, (col_r % 8).astype(F32), -2.0)
    for p in range(3):
        if p == 0:
            expert = second * 32 + first * 8 + x * 2 + c
        elif p == 1:
            expert = second * 32 + y * 8 + first * 2 + c
        else:
            expert = z * 32 + second * 8 + first * 2 + c
        spread = (row_e == expert).astype(F32).astype(BF)

        def make(a, carry, p=p, spread=spread):
            both = meta[p][a].reshape(128, 256)
            ranks = jnp.dot(both[:, :128], spread, preferred_element_type=F32)
            weight = jnp.dot(both[:, 128:], spread, preferred_element_type=F32)
            hit = ranks == slot
            com_s[p, a] = jnp.where(hit, weight, 0.0).astype(BF)
            sel_s[p, a] = jnp.where(hit, 1.0, 0.0).T.astype(BF)
            return carry

        lax.fori_loop(0, 4, make, 0)

    for copy, d in zip(w_in, (2, 1, 3)):
        copy.wait_recv()
        got = w_s.at[(y - d + 4) % 4, c]
        wf_in.append(send(got, got, wf_ss.at[d], wf_rs.at[d], dev(at, other)))
    for copy in at_in:
        copy.wait_recv()
    for copy in wf_in:
        copy.wait_recv()
    lhs = jnp.concatenate(
        [at_r[i // 2, i % 2].reshape(256, 128) for i in range(8)], axis=1
    )
    rs_in = []
    for b in range(CB):
        part = jnp.dot(
            lhs, w_s[:, :, :, b * CBW : (b + 1) * CBW].reshape(1024, CBW), preferred_element_type=F32
        ).reshape(4, 64, CBW)
        pf_s[b] = part
        rs_s[b] = part.astype(BF)
        for d in (2, 1, 3):
            i = b * 4 + d
            rs_in.append(
                send(rs_s.at[b, (x + d) % 4], rs_r.at[b, x], rs_ss.at[i], rs_rs.at[i], dev(along(0, d), c))
            )
    for copy in rs_in:
        copy.wait_recv()
    square = jnp.zeros((64, 1), F32)
    for b in range(CB):
        total = pf_s[b, x]
        for d in (1, 2, 3):
            total = total + rs_r[b, (x - d + 4) % 4].astype(F32)
        pj_s[:, b * CBW : (b + 1) * CBW] = total
        square = square + jnp.sum(total * total, axis=-1, keepdims=True)
    scale = lax.rsqrt(square / 2048.0 + 1e-06)

    line_in = {}
    for p in range(3):
        line[p][at[p], c] = (pj_s[:, OFF[p] : OFF[p] + COLS[p]] * scale).astype(BF)
    for i in (1, 2, 6, 3, 7, 4, 5):
        d, k = i // 2, i % 2
        for p in range(3):
            own = line[p].at[at[p], c]
            line_in[p, i] = send(
                own, own, l_ss.at[p * 8 + i], l_rs.at[p * 8 + i], dev(along(p, d), other if k else c)
            )
    for d in (0, 1, 3, 2):
        for p in range(3):
            source = (at[p] - d + 4) % 4
            for k in range(2):
                if (d, k) != (0, 0):
                    line_in[p, d * 2 + k].wait_recv()
            picked = jnp.dot(
                sel_s[p, source], line[p][source].reshape(128, COLS[p]), preferred_element_type=F32
            )
            ds[p][source] = picked.astype(BF).reshape(16, 16, COLS[p])

    def across(ref, p, first, second):
        return (
            ref.at[:, first, second] if p == 0 else ref.at[first, :, second] if p == 1 else ref.at[first, second]
        )

    d_in = []
    own_copies = []
    here = [(at[PLANE[p][0]], at[PLANE[p][1]]) for p in range(3)]
    for p in range(3):
        copy = pltpu.make_async_copy(
            ds[p].at[:, here[p][0] * 4 + here[p][1]], across(rr[p], p, *here[p]), d_rs.at[p * 16]
        )
        copy.start()
        own_copies.append(copy)

    def plane_target(p, i):
        a, b = i // 4, i % 4
        first, second = (here[p][0] + a) % 4, (here[p][1] + b) % 4
        coords = [None] * 3
        coords[p] = at[p]
        coords[PLANE[p][0]], coords[PLANE[p][1]] = first, second
        return first, second, dev(coords, c)

    for i in ORDER:
        for p in range(3):
            first, second, device = plane_target(p, i)
            d_in.append(
                send(
                    ds[p].at[:, first * 4 + second], across(rr[p], p, *here[p]),
                    d_ss.at[p * 16 + i], d_rs.at[p * 16 + i], device,
                )
            )
    for copy in loads[4:]:
        copy.wait()
    for copy in own_copies:
        copy.wait()
    for copy in d_in:
        copy.wait_recv()

    def expert_rows(step, carry):
        block = (x + step) % 4
        rows = [rr[p][block].reshape(256, COLS[p]) for p in range(3)]
        gate_val = jnp.zeros((256, 768), F32)
        up_val = jnp.zeros((256, 768), F32)
        for p in range(3):
            gate_val = gate_val + jnp.dot(
                rows[p], wg_s[OFF[p] : OFF[p] + COLS[p]], preferred_element_type=F32
            )
            up_val = up_val + jnp.dot(
                rows[p], wu_s[OFF[p] : OFF[p] + COLS[p]], preferred_element_type=F32
            )
        act = (gate_val / (1.0 + jnp.exp(-gate_val)) * up_val).astype(BF)
        for p in range(3):
            result = jnp.dot(act, wd_s[:, OFF[p] : OFF[p] + COLS[p]], preferred_element_type=F32)
            oo[p][block] = result.astype(BF).reshape(4, 4, 16, COLS[p])
        return carry

    lax.fori_loop(0, 4, expert_rows, 0)

    own_copies = []
    e_in = []
    for p in range(3):
        copy = pltpu.make_async_copy(
            across(oo[p], p, *here[p]), rt[p].at[:, here[p][0] * 4 + here[p][1]], e_rs.at[p * 16]
        )
        copy.start()
        own_copies.append(copy)
    for i in ORDER:
        for p in range(3):
            first, second, device = plane_target(p, i)
            e_in.append(
                send(
                    across(oo[p], p, first, second), rt[p].at[:, here[p][0] * 4 + here[p][1]],
                    e_ss.at[p * 16 + i], e_rs.at[p * 16 + i], device,
                )
            )
    for copy in own_copies:
        copy.wait()
    for copy in e_in:
        copy.wait_recv()

    p_in = []
    for d in (2, 1, 3, 0):
        for p in range(3):
            to = (at[p] + d) % 4
            sums = jnp.dot(
                com_s[p, to], rt[p][to].reshape(256, COLS[p]), preferred_element_type=F32
            )
            ps[p][to] = sums.astype(BF).reshape(2, 64, COLS[p])
            for k in range(2):
                if (d, k) != (0, 0):
                    i = d * 2 + k
                    core = other if k else c
                    p_in.append(
                        send(
                            ps[p].at[to, core], pr[p].at[at[p], c], p_ss.at[p * 8 + i], p_rs.at[p * 8 + i],
                            dev(along(p, d), core),
                        )
                    )
    for p in range(3):
        pr[p][at[p], c] = ps[p][at[p], c]
    for copy in p_in:
        copy.wait_recv()
    for p in range(3):
        columns = slice(OFF[p], OFF[p] + COLS[p])
        total = pj_s[:, columns]
        for a in range(4):
            for k in range(2):
                total = total + pr[p][a, k].astype(F32)
        out_ref[:, columns] = total
    for copy in sent:
        copy.wait_send()


def layer(queries, key_rows, values, out_weight, expert_ids, gate_ints, w_gate, w_up, w_down):
    count = queries.shape[0] // CHUNK
    blocks = [a.reshape(count, CHUNK, 128) for a in (queries, key_rows, values)]
    vm = pltpu.VMEM
    sem = lambda n: pltpu.SemaphoreType.DMA((n,))
    by = lambda *lead: [vm((*lead, n), BF) for n in COLS]
    scratch = [
        vm((count, CHUNK, 128), F32), vm((count, CHUNK, 128), F32), vm((count, CHUNK, 128), F32),
        vm((count, CHUNK, 128), F32), vm((128, 128), BF), vm((4, 128, 128), BF),
        vm((4, 2, 4, 64, 128), BF), vm((4, 2, 4, 64, 128), BF), vm((4, 2, 128, 2048), BF),
        vm((CB, 4, 64, CBW), BF), vm((CB, 4, 64, CBW), BF), vm((CB, 4, 64, CBW), F32), vm((64, 2048), F32),
        vm((64, 256), BF), vm((4, 2, 64, 256), BF), vm((4, 2, 64, 256), BF), vm((4, 2, 64, 256), BF),
        vm((3, 4, 256, 128), BF), vm((3, 4, 128, 256), BF),
        *by(4, 2, 64), *by(4, 16, 16), *by(4, 4, 4, 16), *by(4, 4, 4, 16), *by(4, 16, 16),
        *by(4, 2, 64), *by(4, 2, 64),
        vm((2048, 768), BF), vm((2048, 768), BF), vm((768, 2048), BF),
        sem(7), sem(4), sem(4), sem(8), sem(8), sem(4), sem(4), sem(4), sem(4), sem(16), sem(16),
        sem(24), sem(24), sem(24), sem(24), sem(48), sem(48), sem(48), sem(48), sem(24), sem(24),
    ]
    hbm = pl.BlockSpec(memory_space=pl.ANY)
    vmem = pl.BlockSpec(memory_space=pltpu.VMEM)
    return pl.pallas_call(
        body,
        out_shape=jax.ShapeDtypeStruct((64, 2048), F32),
        in_specs=[hbm, hbm, hbm, hbm, vmem, vmem, hbm, hbm, hbm],
        out_specs=vmem,
        scratch_shapes=scratch,
        compiler_params=pltpu.CompilerParams(
            collective_id=0, has_side_effects=True, vmem_limit_bytes=62 << 20
        ),
        cost_estimate=pl.CostEstimate(flops=13 * 10**9, bytes_accessed=14 * 10**6, transcendentals=10**6),
    )(*blocks, out_weight, expert_ids, gate_ints, w_gate[0], w_up[0], w_down[0])


def solution(mesh):
    placed = (
        P("seq", "head"),
        P("seq", "head"),
        P("seq", "head"),
        P("head", None),
        P(("seq", "head"), None),
        P(("seq", "head"), None),
        P(("seq", "head"), None, None),
        P(("seq", "head"), None, None),
        P(("seq", "head"), None, None),
    )
    return jax.shard_map(
        layer, mesh=mesh, in_specs=placed, out_specs=P(("seq", "head"), None), check_vma=False
    )
```

time: 278 us -> 178 us (0.64)
  Pallas kernels: 0 us -> 173 us
  blocking collectives: 70.3 us -> 0 us
  waiting for transfers between devices: 68.5 us -> 0 us
  matrix products: 60 us -> 0 us
  local copies, waits for them, and re-layouts: 36.1 us -> 4.63 us
  starting transfers between devices: 16.8 us -> 0 us
  between operations: 13.6 us -> 0.01 us
  other arithmetic: 9.54 us -> 0 us
    pallas_call x0 -> x1, Pallas kernels: none -> 173 us  [layer(): pl.pallas_call(body, out_shape=jax.ShapeDtypeStruct((64, 2048), F32), in_...]
    all_to_all x2 -> x0, waiting for transfers between devices: 61.4 us -> none  [the longest x1 51.4 us: exchange_both(): lax.all_to_all(blocks, axis, split_axis=0, concat_axis=0, tiled=True)]
    dot_general x20 -> x0, matrix products: 60 us -> none  [the longest x1 12.3 us: shards(): jnp.einsum('nesf,efd->nesd', act, w_down, preferred_element_type=jnp.floa...]
    all_to_all x1 -> x0, blocking collectives: 59.2 us -> none  [exchange_both(): lax.all_to_all(blocks, axis, split_axis=0, concat_axis=0, tiled=True)]
    all_to_all x2 -> x0, starting transfers between devices: 16.7 us -> none  [the longest x1 9.89 us: shards(): lax.all_to_all(attn, 'head', split_axis=0, concat_axis=1, tiled=True)]
    gather x2 -> x0, local copies, waits for them, and re-layouts: 14 us -> none  [the longest x1 8 us: shards(): returned[slot_index].astype(jnp.float32) * gates.reshape(-1)[:, None]]
    all_gather x1 -> x0, blocking collectives: 11.2 us -> none  [shards(): lax.all_gather(local_state[None].astype(jnp.bfloat16), 'seq', axis=0, til...]
    another operation x5 -> x0, local copies, waits for them, and re-layouts: 9.08 us -> none  [the longest x1 6.45 us: exchange_both(): blocks = blocks.reshape(-1, *inside)]
  transfers between devices with their start and end apart: 3 -> 0, of which waited for: 3 -> 0; matrix products, arithmetic and copies ran while one was open for 17% -> 0% of each run, Pallas kernels for 0% -> 0%
where the time goes in v1:
time: 178 us; the launch traced here: 177 us
  Pallas kernels  173 us (97%)
  local copies, waits for them, and re-layouts  4.63 us (3%)
    pallas_call x1, Pallas kernels, layer(): pl.pallas_call(body, out_shape=jax.ShapeDtypeStruct((64, 2048), F32), in_...  173 us
    unnamed x3, local copies, waits for them, and re-layouts  4.63 us

profile of v1, /device:TPU:3, one launch (start us, length us, event | category | flops | bytes accessed | tf_op | source)
XLA Modules:
  0.0 177.3 jit_solution(9647408320060595391)
XLA Ops:
  0.0 1.4 copy.10.ids_ref
  1.4 1.4 copy.11.gi_ref
  2.8 172.7 %shard_map.91 = f32[64,2048]{1,0:T(8,128)} custom-call(f32[8,256,128]{2,1,0:T(8,128)} %bitcast.9, f32[8,256,128]{2,1,0:T(8,128)} %bitcast.10, f32[8,256,128]{2,1,0:T(8,128)} %bitcast.11, bf16[128,2048]{1,0:T(8,128)(2,1)} %w_h.1, s32[64,8]{1,0:T(8,128)} %copy.10.ids_ref, s32[64,8]{1,0:T(8,128)} %copy.11.gi_ref, bf16[2048,768]{1,0:T(8,128)(2,1)} %bitcast.6, ...), custom_call_target="tpu_custom_call" | custom-call | flops 12999999488 | bytes 14000000 | tf_op jit(solution)/shard_map/pallas_call | solution.py:385
  175.4 1.9 %copy.13 = f32[64,2048]{1,0:T(8,128)} copy(f32[64,2048]{1,0:T(8,128)} %shard_map.91) | data formatting | bytes 1048576

commit v2 on v1

v2 whole, which is shorter than its diff:
```python
import functools

import jax
import jax.numpy as jnp
from jax import lax
from jax.experimental import pallas as pl
from jax.experimental.pallas import tpu as pltpu
from jax.sharding import PartitionSpec as P

MESH = pl.DeviceIdType.MESH
BF = jnp.bfloat16
F32 = jnp.float32
COLS = (768, 640, 640)
OFF = (0, 768, 1408)
PLANE = ((1, 2), (0, 2), (0, 1))
ORDER = (5, 10, 15, 8, 2, 7, 13, 1, 4, 11, 14, 3, 12, 6, 9)
CB = 4
CBW = 512
HALF = 1024
STEPS = (0, 1, 2, 3)
CHUNK = 256


def partners():
    found = []
    for a in range(4):
        for b in range(4):
            for d in range(4):
                if 0 in (a, b, d) and (a, b, d) != (0, 0, 0):
                    found.append((a, b, d, 0))
    found.append((0, 0, 0, 1))
    for a in range(1, 4):
        found += [(a, 0, 0, 1), (0, a, 0, 1), (0, 0, a, 1)]
    return found


def body(
    q_h, k_h, v_h, w_h, ids_ref, gi_ref, wg_h, wu_h, wd_h, out_ref,
    q_s, k_s, v_s, o_s, st_s, st_r, at_s, ar0, ar1, w0, w1, rs_s, rs_r, pf_s, pj_s,
    vg_s, m0, m1, m2, sel_s, com_s, l0, l1, l2, ds0, ds1, ds2, r0, r1, r2,
    o0, o1, o2, rt0, rt1, rt2, pf0, pf1, pf2, px0, px1, px2, xr0, xr1, xr2,
    ps0, ps1, ps2, pr0, pr1, pr2, wg_s, wu_s, wd_s,
    loc_sem, st_ss, st_rs, at_ss, at_rs, w_ss, w_rs, wf_ss, wf_rs, rs_ss, rs_rs,
    m_ss, m_rs, l_ss, l_rs, d0_ss, d0_rs, d1_ss, d1_rs, d2_ss, d2_rs,
    e0_ss, e0_rs, e1_ss, e1_rs, e2_ss, e2_rs, x_ss, x_rs, p_ss, p_rs,
):
    meta, line = (m0, m1, m2), (l0, l1, l2)
    ds, rr, oo, rt = (ds0, ds1, ds2), (r0, r1, r2), (o0, o1, o2), (rt0, rt1, rt2)
    pf, px, xr, ps, pr = (pf0, pf1, pf2), (px0, px1, px2), (xr0, xr1, xr2), (ps0, ps1, ps2), (pr0, pr1, pr2)
    ar, ws = (ar0, ar1), (w0, w1)
    z = lax.axis_index("seq")
    head = lax.axis_index("head")
    y, x, c = head // 8, (head // 2) % 4, head % 2
    at = (x, y, z)
    other = 1 - c

    def dev(coords, core):
        return (coords[2], (coords[1] * 4 + coords[0]) * 2 + core)

    def moved(**shift):
        return tuple((at[i] + shift.get("xyz"[i], 0)) % 4 for i in range(3))

    def along(axis, d):
        return tuple((at[i] + d) % 4 if i == axis else at[i] for i in range(3))

    sent = []

    def remote(src, dst, ss, rs, device):
        return pltpu.make_async_remote_copy(
            src_ref=src, dst_ref=dst, send_sem=ss, recv_sem=rs, device_id=device, device_id_type=MESH
        )

    def send(*what):
        copy = remote(*what)
        copy.start()
        sent.append(copy)
        return copy

    loads = []
    for i, (src, dst) in enumerate(
        (
            (k_h, k_s), (v_h, v_s), (w_h.at[:, :HALF], w0.at[y, c]), (w_h.at[:, HALF:], w1.at[x, c]),
            (q_h, q_s), (wg_h, wg_s), (wu_h, wu_s), (wd_h, wd_s),
        )
    ):
        copy = pltpu.make_async_copy(src, dst, loc_sem.at[i])
        copy.start()
        loads.append(copy)

    barrier = pltpu.get_barrier_semaphore()
    greeted = partners()
    for dx, dy, dz, dc in greeted:
        core = other if dc else c
        pl.semaphore_signal(
            barrier, inc=1, device_id=dev(moved(x=dx, y=dy, z=dz), core), device_id_type=MESH
        )

    experts = lax.broadcasted_iota(jnp.int32, (64, 128), 1)
    named = jnp.zeros((64, 128), F32)
    gate = jnp.zeros((64, 128), F32)
    gates = gi_ref[...].astype(F32)
    gates = gates / jnp.sum(gates, axis=-1, keepdims=True)
    for k in range(8):
        hit = ids_ref[:, k : k + 1] == experts
        named = jnp.where(hit, 1.0, named)
        gate = jnp.where(hit, gates[:, k : k + 1], gate)
    before = (
        lax.broadcasted_iota(jnp.int32, (64, 64), 1) < lax.broadcasted_iota(jnp.int32, (64, 64), 0)
    ).astype(F32).astype(BF)
    rank = jnp.dot(before, named.astype(BF), preferred_element_type=F32)
    vg_s[:, :128] = jnp.where(named > 0.5, rank, -1.0).astype(BF)
    vg_s[:, 128:] = gate.astype(BF)

    loads[0].wait()
    loads[1].wait()
    count = q_s.shape[0]
    state = jnp.zeros((128, 128), F32)
    prefix = []
    for i in range(count):
        prefix.append(state)
        state = state + lax.dot_general(
            k_s[i].astype(BF), v_s[i].astype(BF), (((0,), (0,)), ((), ())), preferred_element_type=F32
        )
    st_s[...] = state.astype(BF)
    loads[2].wait()
    loads[3].wait()

    pl.semaphore_wait(barrier, len(greeted))

    st_in = [
        send(st_s, st_r.at[z], st_ss.at[d], st_rs.at[d], dev(along(2, d), c)) for d in (1, 2, 3)
    ]
    w_in, wf_in = {}, []
    lines = (1, 0)
    for d in (2, 1, 3):
        for v in range(2):
            mine = ws[v].at[at[lines[v]], c]
            w_in[v, d] = send(mine, mine, w_ss.at[v * 4 + d], w_rs.at[v * 4 + d], dev(along(lines[v], d), c))
    for v in range(2):
        mine = ws[v].at[at[lines[v]], c]
        wf_in.append(send(mine, mine, wf_ss.at[v * 4], wf_rs.at[v * 4], dev(at, other)))
    meta_in = []
    for p in range(3):
        meta[p][at[p], c] = vg_s[...]
        for i in range(1, 8):
            d, k = i // 2, i % 2
            meta_in.append(
                send(
                    vg_s, meta[p].at[at[p], c], m_ss.at[p * 8 + i], m_rs.at[p * 8 + i],
                    dev(along(p, d), other if k else c),
                )
            )

    loads[4].wait()
    lower = lax.broadcasted_iota(jnp.int32, (CHUNK, CHUNK), 1) <= lax.broadcasted_iota(
        jnp.int32, (CHUNK, CHUNK), 0
    )
    for i in range(count):
        qb, kb = q_s[i].astype(BF), k_s[i].astype(BF)
        scores = lax.dot_general(qb, kb, (((1,), (1,)), ((), ())), preferred_element_type=F32)
        scores = jnp.where(lower, scores, 0.0).astype(BF)
        o_s[i] = jnp.dot(scores, v_s[i].astype(BF), preferred_element_type=F32)
    for copy in st_in:
        copy.wait_recv()
    earlier = jnp.zeros((128, 128), F32)
    for d in (1, 2, 3):
        source = (z - d + 4) % 4
        earlier = earlier + jnp.where(source < z, st_r[source].astype(F32), 0.0)
    for i in range(count):
        total = (prefix[i] + earlier).astype(BF)
        mixed = o_s[i] + jnp.dot(q_s[i].astype(BF), total, preferred_element_type=F32)
        mixed = mixed * lax.rsqrt(jnp.mean(mixed * mixed, axis=-1, keepdims=True) + 1e-06)
        mixed = mixed.astype(BF)
        for j in range(2):
            for k in range(2):
                at_s[i // 2, k, (i % 2) * 2 + j] = mixed[(2 * j + k) * 64 : (2 * j + k + 1) * 64]
    at_in = []
    for i in (4, 5, 2, 3, 6, 7, 1):
        d, k = i // 2, i % 2
        core = other if k else c
        for v in range(2):
            to = (at[lines[v]] + d) % 4
            src = at_s.at[to, core] if v == 0 else at_s.at[:, core, to]
            at_in.append(
                send(
                    src, ar[v].at[at[lines[v]], c], at_ss.at[v * 8 + i], at_rs.at[v * 8 + i],
                    dev(along(lines[v], d), core),
                )
            )
    ar0[y, c] = at_s[y, c]
    ar1[x, c] = at_s[:, c, x]

    for copy in meta_in:
        copy.wait_recv()
    row_e = lax.broadcasted_iota(jnp.int32, (128, 256), 0)
    col_r = lax.broadcasted_iota(jnp.int32, (128, 256), 1)
    first, second = col_r // 64, (col_r // 16) % 4
    same = (row_e // 64) == ((col_r // 8) % 2)
    slot = jnp.where(same, (col_r % 8).astype(F32), -2.0)
    for p in range(3):
        if p == 0:
            expert = second * 32 + first * 8 + x * 2 + c
        elif p == 1:
            expert = second * 32 + y * 8 + first * 2 + c
        else:
            expert = z * 32 + second * 8 + first * 2 + c
        spread = (row_e == expert).astype(F32).astype(BF)

        def make(a, carry, p=p, spread=spread):
            both = meta[p][a].reshape(128, 256)
            ranks = jnp.dot(both[:, :128], spread, preferred_element_type=F32)
            weight = jnp.dot(both[:, 128:], spread, preferred_element_type=F32)
            hit = ranks == slot
            com_s[p, a] = jnp.where(hit, weight, 0.0).astype(BF)
            sel_s[p, a] = jnp.where(hit, 1.0, 0.0).T.astype(BF)
            return carry

        lax.fori_loop(0, 4, make, 0)

    for d in (1, 3, 2):
        for v in range(2):
            w_in[v, d].wait_recv()
            got = ws[v].at[(at[lines[v]] - d + 4) % 4, c]
            wf_in.append(send(got, got, wf_ss.at[v * 4 + d], wf_rs.at[v * 4 + d], dev(at, other)))
    for copy in at_in:
        copy.wait_recv()
    for copy in wf_in:
        copy.wait_recv()
    lhs = [
        jnp.concatenate([ar[v][i // 2, i % 2].reshape(256, 128) for i in range(8)], axis=1)
        for v in range(2)
    ]
    rs_in = []
    for b in range(CB):
        v, low = b % 2, (b // 2) * CBW
        part = jnp.dot(
            lhs[v], ws[v][:, :, :, low : low + CBW].reshape(1024, CBW), preferred_element_type=F32
        ).reshape(4, 64, CBW)
        pf_s[b] = part
        rs_s[b] = part.astype(BF)
        for d in (2, 1, 3):
            i = b * 4 + d
            rs_in.append(
                send(
                    rs_s.at[b, (at[v] + d) % 4], rs_r.at[b, at[v]], rs_ss.at[i], rs_rs.at[i],
                    dev(along(v, d), c),
                )
            )
    for copy in rs_in:
        copy.wait_recv()
    square = jnp.zeros((64, 1), F32)
    for b in range(CB):
        v, low = b % 2, (b % 2) * HALF + (b // 2) * CBW
        total = pf_s[b, at[v]]
        for d in (1, 2, 3):
            total = total + rs_r[b, (at[v] - d + 4) % 4].astype(F32)
        pj_s[:, low : low + CBW] = total
        square = square + jnp.sum(total * total, axis=-1, keepdims=True)
    scale = lax.rsqrt(square / 2048.0 + 1e-06)

    line_in = {}
    for p in range(3):
        line[p][at[p], c] = (pj_s[:, OFF[p] : OFF[p] + COLS[p]] * scale).astype(BF)

    def pass_on(p, d):
        block = line[p].at[(at[p] - d + 4) % 4, c]
        i = p * 8 + d * 2 + 1
        line_in[p, d * 2 + 1] = send(block, block, l_ss.at[i], l_rs.at[i], dev(at, other))

    for d in (2, 1, 3):
        for p in (1, 2, 0):
            own = line[p].at[at[p], c]
            i = p * 8 + d * 2
            line_in[p, d * 2] = send(own, own, l_ss.at[i], l_rs.at[i], dev(along(p, d), c))
    for p in (1, 2, 0):
        pass_on(p, 0)
    for d in (1, 3, 2):
        for p in (1, 2, 0):
            line_in[p, d * 2].wait_recv()
            pass_on(p, d)

    here = [at[PLANE[p][0]] * 4 + at[PLANE[p][1]] for p in range(3)]

    def pick(p, d):
        source = (at[p] - d + 4) % 4
        line_in[p, d * 2 + 1].wait_recv()
        picked = jnp.dot(
            sel_s[p, source], line[p][source].reshape(128, COLS[p]), preferred_element_type=F32
        )
        ds[p][source] = picked.astype(BF).reshape(16, 16, COLS[p])

    def out0(i, k):
        a, first, second = (x + i) % 4, (y + k // 4) % 4, (z + k % 4) % 4
        j = i * 16 + k
        return ds0.at[a, first * 4 + second], r0.at[a, y, z], d0_ss.at[j], d0_rs.at[j], dev((x, first, second), c)

    def out1(i, b):
        first, second = (x + 4 - i) % 4, (z + b) % 4
        j = i * 4 + b
        return ds1.at[:, first * 4 + second], r1.at[x, :, z], d1_ss.at[j], d1_rs.at[j], dev((first, y, second), c)

    def out2(i, b):
        first, second = (x + 4 - i) % 4, (y + b) % 4
        j = i * 4 + b
        return ds2.at[:, first * 4 + second], r2.at[x, y], d2_ss.at[j], d2_rs.at[j], dev((first, second, z), c)

    def back0(i, k):
        a, first, second = (x + i) % 4, (y + k // 4) % 4, (z + k % 4) % 4
        j = i * 16 + k
        return o0.at[a, first, second], rt0.at[a, y * 4 + z], e0_ss.at[j], e0_rs.at[j], dev((x, first, second), c)

    def back1(i, b):
        first, second = (x + i) % 4, (z + b) % 4
        j = i * 4 + b
        return o1.at[first, :, second], rt1.at[:, x * 4 + z], e1_ss.at[j], e1_rs.at[j], dev((first, y, second), c)

    def back2(i, b):
        first, second = (x + i) % 4, (y + b) % 4
        j = i * 4 + b
        return o2.at[first, second], rt2.at[:, x * 4 + y], e2_ss.at[j], e2_rs.at[j], dev((first, second, z), c)

    for d in (0, 1, 3, 2):
        for p in (1, 2):
            pick(p, d)
    r1[x, :, z] = ds1[:, here[1]]
    r2[x, y] = ds2[:, here[2]]
    for i in STEPS:
        pick(0, (4 - i) % 4)
        a = (x + i) % 4
        r0[a, y, z] = ds0[a, here[0]]
        for b in (2, 1, 3, 0):
            if (i, b) != (0, 0):
                send(*out1(i, b))
                send(*out2(i, b))
            for k in ORDER[b * 4 : b * 4 + 4]:
                send(*out0(i, k))
    for copy in loads[5:]:
        copy.wait()

    def expert_rows(turn, carry):
        step = (turn + STEPS[0]) % 4
        block = (x + step) % 4
        for k in range(1, 16):
            remote(*out0(step, k)).wait_recv()
        for b in range(1, 4):
            remote(*out1(step, b)).wait_recv()
            remote(*out2(step, b)).wait_recv()

        @pl.when(step != 0)
        def _():
            remote(*out1(step, 0)).wait_recv()
            remote(*out2(step, 0)).wait_recv()

        rows = [rr[p][block].reshape(256, COLS[p]) for p in range(3)]
        gate_val = jnp.zeros((256, 768), F32)
        up_val = jnp.zeros((256, 768), F32)
        for p in range(3):
            gate_val = gate_val + jnp.dot(
                rows[p], wg_s[OFF[p] : OFF[p] + COLS[p]], preferred_element_type=F32
            )
            up_val = up_val + jnp.dot(
                rows[p], wu_s[OFF[p] : OFF[p] + COLS[p]], preferred_element_type=F32
            )
        act = (gate_val / (1.0 + jnp.exp(-gate_val)) * up_val).astype(BF)
        for p in range(3):
            result = jnp.dot(act, wd_s[:, OFF[p] : OFF[p] + COLS[p]], preferred_element_type=F32)
            oo[p][block] = result.astype(BF).reshape(4, 4, 16, COLS[p])
        rt0[block, here[0]] = o0[block, y, z]
        for b in (2, 1, 3):
            remote(*back1(step, b)).start()
            remote(*back2(step, b)).start()
            for k in ORDER[b * 4 : b * 4 + 4]:
                remote(*back0(step, k)).start()
        for k in ORDER[:4]:
            remote(*back0(step, k)).start()

        @pl.when(step != 0)
        def _():
            remote(*back1(step, 0)).start()
            remote(*back2(step, 0)).start()

        @pl.when(step == 0)
        def _():
            rt1[:, here[1]] = o1[x, :, z]
            rt2[:, here[2]] = o2[x, y]

        return carry

    lax.fori_loop(0, 4, expert_rows, 0)

    x_in, p_in = {}, []

    def combine(p, d):
        to = (at[p] + d) % 4
        sums = jnp.dot(
            com_s[p, to], rt[p][to].reshape(256, COLS[p]), preferred_element_type=F32
        ).reshape(2, 64, COLS[p])
        pf[p][d] = jnp.where(c == 0, sums[0], sums[1])
        px[p][d] = jnp.where(c == 0, sums[1], sums[0]).astype(BF)
        i = p * 4 + d
        x_in[p, d] = send(px[p].at[d], xr[p].at[d], x_ss.at[i], x_rs.at[i], dev(at, other))

    def give(p, d):
        x_in[p, d].wait_recv()
        total = pf[p][d] + xr[p][d].astype(F32)
        if d == 0:
            pf[p][d] = total
            return
        ps[p][d] = total.astype(BF)
        i = p * 4 + d
        p_in.append(send(ps[p].at[d], pr[p].at[d], p_ss.at[i], p_rs.at[i], dev(along(p, d), c)))

    for i in STEPS:
        for k in range(1, 16):
            remote(*back0(i, k)).wait_recv()
        combine(0, i)
    for i in range(4):
        for b in range(4):
            if (i, b) != (0, 0):
                remote(*back1(i, b)).wait_recv()
                remote(*back2(i, b)).wait_recv()
    for d in STEPS:
        give(0, d)
    for d in (2, 1, 3, 0):
        for p in (1, 2):
            combine(p, d)
    for d in (2, 1, 3, 0):
        for p in (1, 2):
            give(p, d)
    for copy in p_in:
        copy.wait_recv()
    for p in range(3):
        columns = slice(OFF[p], OFF[p] + COLS[p])
        total = pj_s[:, columns] + pf[p][0]
        for d in range(1, 4):
            total = total + pr[p][d].astype(F32)
        out_ref[:, columns] = total
    for copy in sent:
        copy.wait_send()
    for i in range(4):
        for k in range(1, 16):
            remote(*back0(i, k)).wait_send()
        for b in range(4):
            if (i, b) != (0, 0):
                remote(*back1(i, b)).wait_send()
                remote(*back2(i, b)).wait_send()


def layer(queries, key_rows, values, out_weight, expert_ids, gate_ints, w_gate, w_up, w_down):
    count = queries.shape[0] // CHUNK
    blocks = [a.reshape(count, CHUNK, 128) for a in (queries, key_rows, values)]
    vm = pltpu.VMEM
    sem = lambda n: pltpu.SemaphoreType.DMA((n,))
    by = lambda *lead: [vm((*lead, n), BF) for n in COLS]
    scratch = [
        vm((count, CHUNK, 128), F32), vm((count, CHUNK, 128), F32), vm((count, CHUNK, 128), F32),
        vm((count, CHUNK, 128), F32), vm((128, 128), BF), vm((4, 128, 128), BF),
        vm((4, 2, 4, 64, 128), BF), vm((4, 2, 4, 64, 128), BF), vm((4, 2, 4, 64, 128), BF),
        vm((4, 2, 128, HALF), BF), vm((4, 2, 128, HALF), BF),
        vm((CB, 4, 64, CBW), BF), vm((CB, 4, 64, CBW), BF), vm((CB, 4, 64, CBW), F32), vm((64, 2048), F32),
        vm((64, 256), BF), vm((4, 2, 64, 256), BF), vm((4, 2, 64, 256), BF), vm((4, 2, 64, 256), BF),
        vm((3, 4, 256, 128), BF), vm((3, 4, 128, 256), BF),
        *by(4, 2, 64), *by(4, 16, 16), *by(4, 4, 4, 16), *by(4, 4, 4, 16), *by(4, 16, 16),
        *[vm((4, 64, n), F32) for n in COLS], *by(4, 64), *by(4, 64), *by(4, 64), *by(4, 64),
        vm((2048, 768), BF), vm((2048, 768), BF), vm((768, 2048), BF),
        sem(8), sem(4), sem(4), sem(16), sem(16), sem(8), sem(8), sem(8), sem(8), sem(16), sem(16),
        sem(24), sem(24), sem(24), sem(24), sem(64), sem(64), sem(16), sem(16), sem(16), sem(16),
        sem(64), sem(64), sem(16), sem(16), sem(16), sem(16), sem(12), sem(12), sem(12), sem(12),
    ]
    hbm = pl.BlockSpec(memory_space=pl.ANY)
    vmem = pl.BlockSpec(memory_space=pltpu.VMEM)
    return pl.pallas_call(
        body,
        out_shape=jax.ShapeDtypeStruct((64, 2048), F32),
        in_specs=[hbm, hbm, hbm, hbm, vmem, vmem, hbm, hbm, hbm],
        out_specs=vmem,
        scratch_shapes=scratch,
        compiler_params=pltpu.CompilerParams(
            collective_id=0, has_side_effects=True, vmem_limit_bytes=62 << 20
        ),
        cost_estimate=pl.CostEstimate(flops=13 * 10**9, bytes_accessed=14 * 10**6, transcendentals=10**6),
    )(*blocks, out_weight, expert_ids, gate_ints, w_gate[0], w_up[0], w_down[0])


def solution(mesh):
    placed = (
        P("seq", "head"),
        P("seq", "head"),
        P("seq", "head"),
        P("head", None),
        P(("seq", "head"), None),
        P(("seq", "head"), None),
        P(("seq", "head"), None, None),
        P(("seq", "head"), None, None),
        P(("seq", "head"), None, None),
    )
    return jax.shard_map(
        layer, mesh=mesh, in_specs=placed, out_specs=P(("seq", "head"), None), check_vma=False
    )
```

time: 178 us -> 146 us (0.82)
  the two profiles are of different devices: /device:TPU:3 before, /device:TPU:8 now
where the time goes in v2:
time: 146 us
  Pallas kernels  141 us (97%)
  local copies, waits for them, and re-layouts  4.63 us (3%)
    pallas_call x1, Pallas kernels, layer(): pl.pallas_call(body, out_shape=jax.ShapeDtypeStruct((64, 2048), F32), in_...  141 us
    unnamed x3, local copies, waits for them, and re-layouts  4.63 us

profile of v2, /device:TPU:8, one launch (start us, length us, event | category | flops | bytes accessed | tf_op | source)
XLA Modules:
  0.0 146.1 jit_solution(1107412757411048973)
XLA Ops:
  0.0 1.4 copy.10.ids_ref
  1.4 1.4 copy.11.gi_ref
  2.8 141.5 %shard_map.91 = f32[64,2048]{1,0:T(8,128)} custom-call(f32[8,256,128]{2,1,0:T(8,128)} %bitcast.9, f32[8,256,128]{2,1,0:T(8,128)} %bitcast.10, f32[8,256,128]{2,1,0:T(8,128)} %bitcast.11, bf16[128,2048]{1,0:T(8,128)(2,1)} %w_h.1, s32[64,8]{1,0:T(8,128)} %copy.10.ids_ref, s32[64,8]{1,0:T(8,128)} %copy.11.gi_ref, bf16[2048,768]{1,0:T(8,128)(2,1)} %bitcast.6, ...), custom_call_target="tpu_custom_call" | custom-call | flops 12999999488 | bytes 14000000 | tf_op jit(solution)/shard_map/pallas_call | solution.py:472
  144.2 1.9 %copy.13 = f32[64,2048]{1,0:T(8,128)} copy(f32[64,2048]{1,0:T(8,128)} %shard_map.91) | data formatting | bytes 1048576

commit v3 on v2

v3 whole, which is shorter than its diff:
```python
import functools

import jax
import jax.numpy as jnp
from jax import lax
from jax.experimental import pallas as pl
from jax.experimental.pallas import tpu as pltpu
from jax.sharding import PartitionSpec as P

MESH = pl.DeviceIdType.MESH
BF = jnp.bfloat16
F32 = jnp.float32
COLS = (768, 640, 640)
OFF = (0, 768, 1408)
PLANE = ((1, 2), (0, 2), (0, 1))
ORDER = (5, 10, 15, 8, 2, 7, 13, 1, 4, 11, 14, 3, 12, 6, 9)
CB = 4
CBW = 512
HALF = 1024
STEPS = (1, 2, 3, 0)
CHUNK = 256


def partners():
    found = []
    for a in range(4):
        for b in range(4):
            for d in range(4):
                if 0 in (a, b, d) and (a, b, d) != (0, 0, 0):
                    found.append((a, b, d, 0))
    found.append((0, 0, 0, 1))
    for a in range(1, 4):
        found += [(a, 0, 0, 1), (0, a, 0, 1), (0, 0, a, 1)]
    return found


def body(
    q_h, k_h, v_h, w_h, ids_ref, gi_ref, wg_h, wu_h, wd_h, out_ref,
    q_s, k_s, v_s, o_s, st_s, st_r, at_s, ar0, ar1, w0, w1, rs_s, rs_r, pf_s, pj_s,
    vg_s, m0, m1, m2, sel_s, com_s, l0, l1, l2, ds0, ds1, ds2, r0, r1, r2,
    o0, o1, o2, rt0, rt1, rt2, pf0, pf1, pf2, px0, px1, px2, xr0, xr1, xr2,
    ps0, ps1, ps2, pr0, pr1, pr2, wg_s, wu_s, wd_s,
    loc_sem, st_ss, st_rs, at_ss, at_rs, w_ss, w_rs, wf_ss, wf_rs, rs_ss, rs_rs,
    m_ss, m_rs, l_ss, l_rs, d_ss, d_rs, e_ss, e_rs, x_ss, x_rs, p_ss, p_rs, q_ss, q_rs, z_ss, z_rs,
):
    meta, line = (m0, m1, m2), (l0, l1, l2)
    ds, rr, oo, rt = (ds0, ds1, ds2), (r0, r1, r2), (o0, o1, o2), (rt0, rt1, rt2)
    pf, px, xr, ps, pr = (pf0, pf1, pf2), (px0, px1, px2), (xr0, xr1, xr2), (ps0, ps1, ps2), (pr0, pr1, pr2)
    ar, ws = (ar0, ar1), (w0, w1)
    z = lax.axis_index("seq")
    head = lax.axis_index("head")
    y, x, c = head // 8, (head // 2) % 4, head % 2
    at = (x, y, z)
    other = 1 - c

    def dev(coords, core):
        return (coords[2], (coords[1] * 4 + coords[0]) * 2 + core)

    def moved(**shift):
        return tuple((at[i] + shift.get("xyz"[i], 0)) % 4 for i in range(3))

    def along(axis, d):
        return tuple((at[i] + d) % 4 if i == axis else at[i] for i in range(3))

    sent = []

    def remote(src, dst, ss, rs, device):
        return pltpu.make_async_remote_copy(
            src_ref=src, dst_ref=dst, send_sem=ss, recv_sem=rs, device_id=device, device_id_type=MESH
        )

    def send(*what):
        copy = remote(*what)
        copy.start()
        sent.append(copy)
        return copy

    loads = []
    for i, (src, dst) in enumerate(
        (
            (k_h, k_s), (v_h, v_s), (w_h.at[:, :HALF], w0.at[y, c]), (w_h.at[:, HALF:], w1.at[x, c]),
            (q_h, q_s), (wg_h, wg_s), (wu_h, wu_s), (wd_h, wd_s),
        )
    ):
        copy = pltpu.make_async_copy(src, dst, loc_sem.at[i])
        copy.start()
        loads.append(copy)

    barrier = pltpu.get_barrier_semaphore()
    greeted = partners()
    for dx, dy, dz, dc in greeted:
        core = other if dc else c
        pl.semaphore_signal(
            barrier, inc=1, device_id=dev(moved(x=dx, y=dy, z=dz), core), device_id_type=MESH
        )

    ids = ids_ref[...]
    experts = lax.broadcasted_iota(jnp.int32, (128, 64), 0)
    gates = gi_ref[...].astype(F32)
    gates = gates / jnp.sum(gates, axis=0, keepdims=True)
    named = jnp.zeros((128, 64), F32)
    for k in range(8):
        named = jnp.where(ids[k : k + 1] == experts, 1.0, named)
    before = (
        lax.broadcasted_iota(jnp.int32, (64, 64), 0) < lax.broadcasted_iota(jnp.int32, (64, 64), 1)
    ).astype(F32).astype(BF)
    rank = jnp.dot(named.astype(BF), before, preferred_element_type=F32)
    ranks = jnp.concatenate(
        [
            jnp.sum(jnp.where(ids[k : k + 1] == experts, rank, 0.0), axis=0, keepdims=True)
            for k in range(8)
        ],
        axis=0,
    )
    upper = jnp.concatenate([ids.astype(F32), gates], axis=1)
    under = jnp.concatenate([ranks, ranks], axis=1)
    vg_s[...] = jnp.concatenate([upper, under], axis=0).astype(BF)

    loads[0].wait()
    loads[1].wait()
    count = q_s.shape[0]
    state = jnp.zeros((128, 128), F32)
    prefix = []
    for i in range(count):
        prefix.append(state)
        state = state + lax.dot_general(
            k_s[i].astype(BF), v_s[i].astype(BF), (((0,), (0,)), ((), ())), preferred_element_type=F32
        )
    st_s[...] = state.astype(BF)
    loads[2].wait()
    loads[3].wait()

    pl.semaphore_wait(barrier, len(greeted))

    st_in = [
        send(st_s, st_r.at[z], st_ss.at[d], st_rs.at[d], dev(along(2, d), c)) for d in (1, 2, 3)
    ]
    lines = (1, 0)

    def straight(v, a):
        return ws[v].at[a, c, :, :CBW]

    def quarter(v, a):
        return ws[v].at[a, c, :, pl.ds(pl.multiple_of(CBW + 128 * z, 128), 128)]

    w_in, q_in, wf_in = {}, {}, {}
    for d in (2, 1, 3):
        for v in range(2):
            i = v * 4 + d
            mine = quarter(v, at[lines[v]])
            q_in[v, d] = send(mine, mine, q_ss.at[i], q_rs.at[i], dev(along(lines[v], d), c))
    for d in (2, 1, 3):
        for v in range(2):
            i = v * 4 + d
            mine = straight(v, at[lines[v]])
            w_in[v, d] = send(mine, mine, w_ss.at[i], w_rs.at[i], dev(along(lines[v], d), c))

    def hand_on(v, d, half):
        got = ws[v].at[(at[lines[v]] - d + 4) % 4, c, :, half * CBW : (half + 1) * CBW]
        i = half * 8 + v * 4 + d
        wf_in[v, d, half] = send(got, got, wf_ss.at[i], wf_rs.at[i], dev(at, other))

    for v in range(2):
        for half in range(2):
            hand_on(v, 0, half)
    meta_in = []
    for p in range(3):
        meta[p][0, c] = vg_s[...]
        for i in range(1, 8):
            d, k = i // 2, i % 2
            meta_in.append(
                send(
                    vg_s, meta[p].at[(4 - d) % 4, c], m_ss.at[p * 8 + i], m_rs.at[p * 8 + i],
                    dev(along(p, d), other if k else c),
                )
            )

    loads[4].wait()
    lower = lax.broadcasted_iota(jnp.int32, (CHUNK, CHUNK), 1) <= lax.broadcasted_iota(
        jnp.int32, (CHUNK, CHUNK), 0
    )
    for i in range(count):
        qb, kb = q_s[i].astype(BF), k_s[i].astype(BF)
        scores = lax.dot_general(qb, kb, (((1,), (1,)), ((), ())), preferred_element_type=F32)
        scores = jnp.where(lower, scores, 0.0).astype(BF)
        o_s[i] = jnp.dot(scores, v_s[i].astype(BF), preferred_element_type=F32)
    z_in = {}
    for d in (1, 3, 2):
        for v in range(2):
            q_in[v, d].wait_recv()
            got = quarter(v, (at[lines[v]] - d + 4) % 4)
            for e in (2, 1, 3):
                i = v * 16 + d * 4 + e
                z_in[v, d, e] = send(got, got, z_ss.at[i], z_rs.at[i], dev(along(2, e), c))
    for copy in st_in:
        copy.wait_recv()
    earlier = jnp.zeros((128, 128), F32)
    for d in (1, 2, 3):
        source = (z - d + 4) % 4
        earlier = earlier + jnp.where(source < z, st_r[source].astype(F32), 0.0)
    for i in range(count):
        total = (prefix[i] + earlier).astype(BF)
        mixed = o_s[i] + jnp.dot(q_s[i].astype(BF), total, preferred_element_type=F32)
        mixed = mixed * lax.rsqrt(jnp.mean(mixed * mixed, axis=-1, keepdims=True) + 1e-06)
        mixed = mixed.astype(BF)
        for j in range(2):
            for k in range(2):
                at_s[i // 2, k, (i % 2) * 2 + j] = mixed[(2 * j + k) * 64 : (2 * j + k + 1) * 64]
    at_in = []
    for i in (4, 5, 2, 3, 6, 7, 1):
        d, k = i // 2, i % 2
        core = other if k else c
        for v in range(2):
            to = (at[lines[v]] + d) % 4
            src = at_s.at[to, core] if v == 0 else at_s.at[:, core, to]
            at_in.append(
                send(
                    src, ar[v].at[at[lines[v]], c], at_ss.at[v * 8 + i], at_rs.at[v * 8 + i],
                    dev(along(lines[v], d), core),
                )
            )
    ar0[y, c] = at_s[y, c]
    ar1[x, c] = at_s[:, c, x]

    for copy in meta_in:
        copy.wait_recv()
    row_r = lax.broadcasted_iota(jnp.int32, (256, 128), 0)
    base = lax.broadcasted_iota(jnp.int32, (8, 128), 1) // 64 * 1024
    first, second = row_r // 64, (row_r // 16) % 4
    for p in range(3):
        one, two = (first + at[PLANE[p][0]]) % 4, (second + at[PLANE[p][1]]) % 4
        if p == 0:
            expert = two * 32 + one * 8 + x * 2 + c
        elif p == 1:
            expert = two * 32 + y * 8 + one * 2 + c
        else:
            expert = z * 32 + two * 8 + one * 2 + c
        wanted = (row_r // 8) % 2 * 1024 + expert * 8 + row_r % 8

        def make(d, carry, p=p, wanted=wanted):
            both = meta[p][d].astype(F32)
            code = jnp.concatenate([both[0, :8, :64], both[1, :8, :64]], axis=1) * 8.0
            code = code + jnp.concatenate([both[0, 8:, :64], both[1, 8:, :64]], axis=1)
            code = code.astype(jnp.int32) + base
            weight = jnp.concatenate([both[0, :8, 64:], both[1, :8, 64:]], axis=1)
            sel = jnp.zeros((256, 128), F32)
            com = jnp.zeros((256, 128), F32)
            for k in range(8):
                hit = code[k : k + 1] == wanted
                sel = jnp.where(hit, 1.0, sel)
                com = jnp.where(hit, weight[k : k + 1], com)
            sel_s[p, d] = sel.astype(BF)
            com_s[p, d] = com.T.astype(BF)
            return carry

        lax.fori_loop(0, 4, make, 0)

    for d in (1, 3, 2):
        for v in range(2):
            w_in[v, d].wait_recv()
            hand_on(v, d, 0)
    for d in (1, 3, 2):
        for v in range(2):
            for e in (1, 2, 3):
                z_in[v, d, e].wait_recv()
            hand_on(v, d, 1)
    for copy in at_in:
        copy.wait_recv()
    lhs = [
        jnp.concatenate([ar[v][i // 2, i % 2].reshape(256, 128) for i in range(8)], axis=1)
        for v in range(2)
    ]
    rs_in = []
    for b in range(CB):
        v, low = b % 2, (b // 2) * CBW
        for d in range(4):
            wf_in[v, d, b // 2].wait_recv()
        part = jnp.dot(
            lhs[v], ws[v][:, :, :, low : low + CBW].reshape(1024, CBW), preferred_element_type=F32
        ).reshape(4, 64, CBW)
        pf_s[b] = part
        rs_s[b] = part.astype(BF)
        for d in (2, 1, 3):
            i = b * 4 + d
            rs_in.append(
                send(
                    rs_s.at[b, (at[v] + d) % 4], rs_r.at[b, at[v]], rs_ss.at[i], rs_rs.at[i],
                    dev(along(v, d), c),
                )
            )
    for copy in rs_in:
        copy.wait_recv()
    square = jnp.zeros((64, 1), F32)
    for b in range(CB):
        v, low = b % 2, (b % 2) * HALF + (b // 2) * CBW
        total = pf_s[b, at[v]]
        for d in (1, 2, 3):
            total = total + rs_r[b, (at[v] - d + 4) % 4].astype(F32)
        pj_s[:, low : low + CBW] = total
        square = square + jnp.sum(total * total, axis=-1, keepdims=True)
    scale = lax.rsqrt(square / 2048.0 + 1e-06)

    line_in = {}
    for p in range(3):
        line[p][0, c] = (pj_s[:, OFF[p] : OFF[p] + COLS[p]] * scale).astype(BF)

    def pass_on(p, d):
        block = line[p].at[(4 - d) % 4, c]
        i = p * 8 + d * 2 + 1
        line_in[p, d * 2 + 1] = send(block, block, l_ss.at[i], l_rs.at[i], dev(at, other))

    for p in (1, 2, 0):
        pass_on(p, 0)
    for d in (2, 1, 3):
        for p in (1, 2, 0):
            own = line[p].at[0, c]
            i = p * 8 + d * 2
            line_in[p, d * 2] = send(
                own, line[p].at[4 - d, c], l_ss.at[i], l_rs.at[i], dev(along(p, d), c)
            )

    def pick(p, rel):
        line_in[p, (4 - rel) % 4 * 2 + 1].wait_recv()
        picked = jnp.dot(
            sel_s[p, rel], line[p][rel].reshape(128, COLS[p]), preferred_element_type=F32
        )
        ds[p][rel] = picked.astype(BF).reshape(16, 16, COLS[p])

    def minus(k):
        return (4 - k // 4) % 4 * 4 + (4 - k % 4) % 4

    def plane_dev(p, k):
        coords = [None] * 3
        coords[p] = at[p]
        coords[PLANE[p][0]] = (at[PLANE[p][0]] + k // 4) % 4
        coords[PLANE[p][1]] = (at[PLANE[p][1]] + k % 4) % 4
        return dev(coords, c)

    def rows(ref, p, part, first, second):
        if p == 0:
            return ref.at[part, first, second]
        which = 0 if part == 0 else slice(1, 4)
        return ref.at[first, which, second] if p == 1 else ref.at[first, second, which]

    def blocks(ref, p, part, k):
        if p == 0 or part == 0:
            return ref.at[part, k]
        return ref.at[1:4, k]

    def out(p, part, k):
        j = part * 16 + k
        n = minus(k)
        return (
            blocks(ds[p], p, part, k), rows(rr[p], p, part, n // 4, n % 4), d_ss.at[p * 64 + j],
            d_rs.at[p * 64 + j], plane_dev(p, k),
        )

    def back(p, part, k):
        j = part * 16 + k
        return (
            rows(oo[p], p, part, k // 4, k % 4), blocks(rt[p], p, part, minus(k)), e_ss.at[p * 64 + j],
            e_rs.at[p * 64 + j], plane_dev(p, k),
        )

    d_in, e_in = {}, {}

    def go(p, part, k):
        d_in[p, part, k] = send(*out(p, part, k))

    for p in (1, 2, 0):
        pick(p, 0)
        for k in ORDER:
            go(p, 0, k)
    for p in range(3):
        if p == 0:
            r0[0, 0, 0] = ds0[0, 0]
        elif p == 1:
            r1[0, 0, 0] = ds1[0, 0]
        else:
            r2[0, 0, 0] = ds2[0, 0]
    for d in (1, 3, 2):
        for p in (1, 2, 0):
            line_in[p, d * 2].wait_recv()
            pass_on(p, d)
    for rel in (3, 1, 2):
        for p in (1, 2):
            pick(p, rel)
    r1[0, 1:4, 0] = ds1[1:4, 0]
    r2[0, 0, 1:4] = ds2[1:4, 0]
    for i in STEPS:
        if i:
            pick(0, i)
            r0[i, 0, 0] = ds0[i, 0]
        for b in (2, 1, 3, 0):
            k = (4 - i) % 4 * 4 + b
            if k:
                go(1, 1, k)
                go(2, 1, k)
            if i:
                for k in ORDER[b * 4 : b * 4 + 4]:
                    go(0, i, k)
    for copy in loads[5:]:
        copy.wait()

    def expert_rows(i):
        taken = [rr[p][i].reshape(256, COLS[p]) for p in range(3)]
        gate_val = jnp.zeros((256, 768), F32)
        up_val = jnp.zeros((256, 768), F32)
        for p in range(3):
            gate_val = gate_val + jnp.dot(
                taken[p], wg_s[OFF[p] : OFF[p] + COLS[p]], preferred_element_type=F32
            )
            up_val = up_val + jnp.dot(
                taken[p], wu_s[OFF[p] : OFF[p] + COLS[p]], preferred_element_type=F32
            )
        act = (gate_val / (1.0 + jnp.exp(-gate_val)) * up_val).astype(BF)
        for p in range(3):
            result = jnp.dot(act, wd_s[:, OFF[p] : OFF[p] + COLS[p]], preferred_element_type=F32)
            oo[p][i] = result.astype(BF).reshape(4, 4, 16, COLS[p])

    def come(p, part, k):
        e_in[p, part, k] = send(*back(p, part, k))

    for i in STEPS:
        for k in range(1, 16):
            d_in[0, i, k].wait_recv()
        for b in range(4):
            k = (4 - i) % 4 * 4 + b
            if k:
                for p in (1, 2):
                    d_in[p, 0, k].wait_recv()
                    d_in[p, 1, k].wait_recv()
        expert_rows(i)
        rt0[i, 0] = o0[i, 0, 0]
        for b in (2, 1, 3, 0):
            k = i * 4 + b
            if k:
                come(1, 1, k)
                come(2, 1, k)
            for k in ORDER[b * 4 : b * 4 + 4]:
                come(0, i, k)
    for k in ORDER:
        for p in (1, 2):
            come(p, 0, k)
    rt1[:, 0] = o1[0, :, 0]
    rt2[:, 0] = o2[0, 0]

    x_in, p_in = {}, []

    def combine(p, d):
        sums = jnp.dot(
            com_s[p, d], rt[p][d].reshape(256, COLS[p]), preferred_element_type=F32
        ).reshape(2, 64, COLS[p])
        pf[p][d] = jnp.where(c == 0, sums[0], sums[1])
        px[p][d] = jnp.where(c == 0, sums[1], sums[0]).astype(BF)
        i = p * 4 + d
        x_in[p, d] = send(px[p].at[d], xr[p].at[d], x_ss.at[i], x_rs.at[i], dev(at, other))

    def give(p, d):
        x_in[p, d].wait_recv()
        total = pf[p][d] + xr[p][d].astype(F32)
        if d == 0:
            pf[p][d] = total
            return
        ps[p][d] = total.astype(BF)
        i = p * 4 + d
        p_in.append(send(ps[p].at[d], pr[p].at[d], p_ss.at[i], p_rs.at[i], dev(along(p, d), c)))

    for i in STEPS[:3]:
        for k in range(1, 16):
            e_in[0, i, k].wait_recv()
        combine(0, i)
    for d in STEPS[:3]:
        give(0, d)
    for k in range(1, 16):
        for p in (1, 2):
            e_in[p, 1, k].wait_recv()
    for d in (2, 1, 3):
        for p in (1, 2):
            combine(p, d)
    for d in (2, 1, 3):
        for p in (1, 2):
            give(p, d)
    for k in range(1, 16):
        e_in[0, 0, k].wait_recv()
    combine(0, 0)
    for p in (1, 2):
        for k in range(1, 16):
            e_in[p, 0, k].wait_recv()
        combine(p, 0)
    for p in range(3):
        give(p, 0)
    for copy in p_in:
        copy.wait_recv()
    for p in range(3):
        columns = slice(OFF[p], OFF[p] + COLS[p])
        total = pj_s[:, columns] + pf[p][0]
        for d in range(1, 4):
            total = total + pr[p][d].astype(F32)
        out_ref[:, columns] = total
    for copy in sent:
        copy.wait_send()


def layer(queries, key_rows, values, out_weight, expert_ids, gate_ints, w_gate, w_up, w_down):
    count = queries.shape[0] // CHUNK
    blocks = [a.reshape(count, CHUNK, 128) for a in (queries, key_rows, values)]
    vm = pltpu.VMEM
    sem = lambda n: pltpu.SemaphoreType.DMA((n,))
    by = lambda *lead: [vm((*lead, n), BF) for n in COLS]
    scratch = [
        vm((count, CHUNK, 128), F32), vm((count, CHUNK, 128), F32), vm((count, CHUNK, 128), F32),
        vm((count, CHUNK, 128), F32), vm((128, 128), BF), vm((4, 128, 128), BF),
        vm((4, 2, 4, 64, 128), BF), vm((4, 2, 4, 64, 128), BF), vm((4, 2, 4, 64, 128), BF),
        vm((4, 2, 128, HALF), BF), vm((4, 2, 128, HALF), BF),
        vm((CB, 4, 64, CBW), BF), vm((CB, 4, 64, CBW), BF), vm((CB, 4, 64, CBW), F32), vm((64, 2048), F32),
        vm((16, 128), BF), vm((4, 2, 16, 128), BF), vm((4, 2, 16, 128), BF), vm((4, 2, 16, 128), BF),
        vm((3, 4, 256, 128), BF), vm((3, 4, 128, 256), BF),
        *by(4, 2, 64), *by(4, 16, 16), *by(4, 4, 4, 16), *by(4, 4, 4, 16), *by(4, 16, 16),
        *[vm((4, 64, n), F32) for n in COLS], *by(4, 64), *by(4, 64), *by(4, 64), *by(4, 64),
        vm((2048, 768), BF), vm((2048, 768), BF), vm((768, 2048), BF),
        sem(8), sem(4), sem(4), sem(16), sem(16), sem(8), sem(8), sem(16), sem(16), sem(16), sem(16),
        sem(24), sem(24), sem(24), sem(24), sem(192), sem(192), sem(192), sem(192),
        sem(12), sem(12), sem(12), sem(12), sem(8), sem(8), sem(32), sem(32),
    ]
    hbm = pl.BlockSpec(memory_space=pl.ANY)
    vmem = pl.BlockSpec(memory_space=pltpu.VMEM)
    return pl.pallas_call(
        body,
        out_shape=jax.ShapeDtypeStruct((64, 2048), F32),
        in_specs=[hbm, hbm, hbm, hbm, vmem, vmem, hbm, hbm, hbm],
        out_specs=vmem,
        scratch_shapes=scratch,
        compiler_params=pltpu.CompilerParams(
            collective_id=0, has_side_effects=True, vmem_limit_bytes=62 << 20
        ),
        cost_estimate=pl.CostEstimate(flops=13 * 10**9, bytes_accessed=14 * 10**6, transcendentals=10**6),
    )(*blocks, out_weight, expert_ids.T, gate_ints.T, w_gate[0], w_up[0], w_down[0])


def solution(mesh):
    placed = (
        P("seq", "head"),
        P("seq", "head"),
        P("seq", "head"),
        P("head", None),
        P(("seq", "head"), None),
        P(("seq", "head"), None),
        P(("seq", "head"), None, None),
        P(("seq", "head"), None, None),
        P(("seq", "head"), None, None),
    )
    return jax.shard_map(
        layer, mesh=mesh, in_specs=placed, out_specs=P(("seq", "head"), None), check_vma=False
    )
```

time: 146 us -> 127 us (0.87)
  the two profiles are of different devices: /device:TPU:8 before, /device:TPU:3 now
where the time goes in v3:
time: 127 us
  Pallas kernels  125 us (98%)
  local copies, waits for them, and re-layouts  1.87 us (1%)
    pallas_call x1, Pallas kernels, layer(): pl.pallas_call(body, out_shape=jax.ShapeDtypeStruct((64, 2048), F32), in_...  125 us

profile of v3, /device:TPU:3, one launch (start us, length us, event | category | flops | bytes accessed | tf_op | source)
XLA Modules:
  0.0 127.3 jit_solution(16180882240738737107)
XLA Ops:
  0.0 125.4 %shard_map.91 = f32[64,2048]{1,0:T(8,128)} custom-call(f32[8,256,128]{2,1,0:T(8,128)} %bitcast.11, f32[8,256,128]{2,1,0:T(8,128)} %bitcast.12, f32[8,256,128]{2,1,0:T(8,128)} %bitcast.13, bf16[128,2048]{1,0:T(8,128)(2,1)} %w_h.1, s32[8,64]{1,0:T(8,128)} %bitcast.14, s32[8,64]{1,0:T(8,128)} %bitcast.15, bf16[2048,768]{1,0:T(8,128)(2,1)} %bitcast.8, ...), custom_call_target="tpu_custom_call" | custom-call | flops 12999999488 | bytes 14000000 | tf_op jit(solution)/shard_map/pallas_call | solution.py:528
  125.4 1.9 %copy.11 = f32[64,2048]{1,0:T(8,128)} copy(f32[64,2048]{1,0:T(8,128)} %shard_map.91) | data formatting | bytes 1048576

commit v4 on v3

--- a/solution.py
+++ b/solution.py
@@ -62,7 +62,7 @@
     def along(axis, d):
         return tuple((at[i] + d) % 4 if i == axis else at[i] for i in range(3))
 
-    sent = []
+    drains = []
 
     def remote(src, dst, ss, rs, device):
         return pltpu.make_async_remote_copy(
@@ -72,8 +72,13 @@
     def send(*what):
         copy = remote(*what)
         copy.start()
-        sent.append(copy)
         return copy
+
+    def arrived(ref, sem):
+        pltpu.make_async_copy(ref, ref, sem).wait()
+
+    def keep(src, dst, sem):
+        pltpu.make_async_copy(src, dst, sem).start()
 
     loads = []
     for i, (src, dst) in enumerate(
@@ -132,9 +137,9 @@
 
     pl.semaphore_wait(barrier, len(greeted))
 
-    st_in = [
-        send(st_s, st_r.at[z], st_ss.at[d], st_rs.at[d], dev(along(2, d), c)) for d in (1, 2, 3)
-    ]
+    for d in (1, 2, 3):
+        send(st_s, st_r.at[z], st_ss.at[0], st_rs.at[0], dev(along(2, d), c))
+    drains.append((st_r.at[1:4], st_ss.at[0]))
     lines = (1, 0)
 
     def straight(v, a):
@@ -143,37 +148,40 @@
     def quarter(v, a):
         return ws[v].at[a, c, :, pl.ds(pl.multiple_of(CBW + 128 * z, 128), 128)]
 
-    w_in, q_in, wf_in = {}, {}, {}
+    w_in, q_in = {}, {}
     for d in (2, 1, 3):
         for v in range(2):
             i = v * 4 + d
             mine = quarter(v, at[lines[v]])
-            q_in[v, d] = send(mine, mine, q_ss.at[i], q_rs.at[i], dev(along(lines[v], d), c))
+            q_in[v, d] = send(mine, mine, q_ss.at[v], q_rs.at[i], dev(along(lines[v], d), c))
     for d in (2, 1, 3):
         for v in range(2):
             i = v * 4 + d
             mine = straight(v, at[lines[v]])
-            w_in[v, d] = send(mine, mine, w_ss.at[i], w_rs.at[i], dev(along(lines[v], d), c))
+            w_in[v, d] = send(mine, mine, w_ss.at[v], w_rs.at[i], dev(along(lines[v], d), c))
 
     def hand_on(v, d, half):
         got = ws[v].at[(at[lines[v]] - d + 4) % 4, c, :, half * CBW : (half + 1) * CBW]
-        i = half * 8 + v * 4 + d
-        wf_in[v, d, half] = send(got, got, wf_ss.at[i], wf_rs.at[i], dev(at, other))
+        i = half * 2 + v
+        send(got, got, wf_ss.at[i], wf_rs.at[i], dev(at, other))
 
     for v in range(2):
         for half in range(2):
             hand_on(v, 0, half)
-    meta_in = []
-    for p in range(3):
-        meta[p][0, c] = vg_s[...]
+            drains.append((ws[v].at[:, 0, :, :CBW], wf_ss.at[half * 2 + v]))
+        drains.append((ws[v].at[1:4, 0, :, :CBW], w_ss.at[v]))
+        drains.append((ws[v].at[1:4, 0, :, :128], q_ss.at[v]))
+        drains.append((ws[v].at[1:4, 0, :, :384], z_ss.at[v]))
+    for p in range(3):
+        keep(vg_s, meta[p].at[0, c], m_rs.at[p])
         for i in range(1, 8):
             d, k = i // 2, i % 2
-            meta_in.append(
-                send(
-                    vg_s, meta[p].at[(4 - d) % 4, c], m_ss.at[p * 8 + i], m_rs.at[p * 8 + i],
-                    dev(along(p, d), other if k else c),
-                )
+            send(
+                vg_s, meta[p].at[(4 - d) % 4, c], m_ss.at[p * 2 + k], m_rs.at[p],
+                dev(along(p, d), other if k else c),
             )
+        drains.append((meta[p].at[1:4, 0], m_ss.at[p * 2]))
+        drains.append((meta[p].at[:, 0], m_ss.at[p * 2 + 1]))
 
     loads[4].wait()
     lower = lax.broadcasted_iota(jnp.int32, (CHUNK, CHUNK), 1) <= lax.broadcasted_iota(
@@ -184,16 +192,13 @@
         scores = lax.dot_general(qb, kb, (((1,), (1,)), ((), ())), preferred_element_type=F32)
         scores = jnp.where(lower, scores, 0.0).astype(BF)
         o_s[i] = jnp.dot(scores, v_s[i].astype(BF), preferred_element_type=F32)
-    z_in = {}
     for d in (1, 3, 2):
         for v in range(2):
             q_in[v, d].wait_recv()
             got = quarter(v, (at[lines[v]] - d + 4) % 4)
             for e in (2, 1, 3):
-                i = v * 16 + d * 4 + e
-                z_in[v, d, e] = send(got, got, z_ss.at[i], z_rs.at[i], dev(along(2, e), c))
-    for copy in st_in:
-        copy.wait_recv()
+                send(got, got, z_ss.at[v], z_rs.at[v * 4 + d], dev(along(2, e), c))
+    arrived(st_r.at[1:4], st_rs.at[0])
     earlier = jnp.zeros((128, 128), F32)
     for d in (1, 2, 3):
         source = (z - d + 4) % 4
@@ -206,24 +211,25 @@
         for j in range(2):
             for k in range(2):
                 at_s[i // 2, k, (i % 2) * 2 + j] = mixed[(2 * j + k) * 64 : (2 * j + k + 1) * 64]
-    at_in = []
+    for v in range(2):
+        own = at_s.at[y, c] if v == 0 else at_s.at[:, c, x]
+        keep(own, ar[v].at[at[lines[v]], c], at_rs.at[v])
     for i in (4, 5, 2, 3, 6, 7, 1):
         d, k = i // 2, i % 2
         core = other if k else c
         for v in range(2):
             to = (at[lines[v]] + d) % 4
             src = at_s.at[to, core] if v == 0 else at_s.at[:, core, to]
-            at_in.append(
-                send(
-                    src, ar[v].at[at[lines[v]], c], at_ss.at[v * 8 + i], at_rs.at[v * 8 + i],
-                    dev(along(lines[v], d), core),
-                )
+            send(
+                src, ar[v].at[at[lines[v]], c], at_ss.at[v if d else 2], at_rs.at[v],
+                dev(along(lines[v], d), core),
             )
-    ar0[y, c] = at_s[y, c]
-    ar1[x, c] = at_s[:, c, x]
-
-    for copy in meta_in:
-        copy.wait_recv()
+    drains.append((ar0.at[1:4], at_ss.at[0]))
+    drains.append((ar1.at[1:4], at_ss.at[1]))
+    drains.append((ar0.at[0], at_ss.at[2]))
+
+    for p in range(3):
+        arrived(meta[p], m_rs.at[p])
     row_r = lax.broadcasted_iota(jnp.int32, (256, 128), 0)
     base = lax.broadcasted_iota(jnp.int32, (8, 128), 1) // 64 * 1024
     first, second = row_r // 64, (row_r // 16) % 4
@@ -261,38 +267,32 @@
             hand_on(v, d, 0)
     for d in (1, 3, 2):
         for v in range(2):
-            for e in (1, 2, 3):
-                z_in[v, d, e].wait_recv()
+            arrived(ws[v].at[0, 0, :, :384], z_rs.at[v * 4 + d])
             hand_on(v, d, 1)
-    for copy in at_in:
-        copy.wait_recv()
+    for v in range(2):
+        arrived(ar[v], at_rs.at[v])
     lhs = [
         jnp.concatenate([ar[v][i // 2, i % 2].reshape(256, 128) for i in range(8)], axis=1)
         for v in range(2)
     ]
-    rs_in = []
     for b in range(CB):
         v, low = b % 2, (b // 2) * CBW
-        for d in range(4):
-            wf_in[v, d, b // 2].wait_recv()
+        arrived(ws[v].at[:, 0, :, :CBW], wf_rs.at[b])
         part = jnp.dot(
             lhs[v], ws[v][:, :, :, low : low + CBW].reshape(1024, CBW), preferred_element_type=F32
         ).reshape(4, 64, CBW)
         pf_s[b] = part
         rs_s[b] = part.astype(BF)
         for d in (2, 1, 3):
-            i = b * 4 + d
-            rs_in.append(
-                send(
-                    rs_s.at[b, (at[v] + d) % 4], rs_r.at[b, at[v]], rs_ss.at[i], rs_rs.at[i],
-                    dev(along(v, d), c),
-                )
+            send(
+                rs_s.at[b, (at[v] + d) % 4], rs_r.at[b, at[v]], rs_ss.at[0], rs_rs.at[b],
+                dev(along(v, d), c),
             )
-    for copy in rs_in:
-        copy.wait_recv()
+    drains.append((rs_r.at[:, 1:4], rs_ss.at[0]))
     square = jnp.zeros((64, 1), F32)
     for b in range(CB):
         v, low = b % 2, (b % 2) * HALF + (b // 2) * CBW
+        arrived(rs_r.at[b, 1:4], rs_rs.at[b])
         total = pf_s[b, at[v]]
         for d in (1, 2, 3):
             total = total + rs_r[b, (at[v] - d + 4) % 4].astype(F32)
@@ -307,7 +307,7 @@
     def pass_on(p, d):
         block = line[p].at[(4 - d) % 4, c]
         i = p * 8 + d * 2 + 1
-        line_in[p, d * 2 + 1] = send(block, block, l_ss.at[i], l_rs.at[i], dev(at, other))
+        line_in[p, d * 2 + 1] = send(block, block, l_ss.at[p * 2 + 1], l_rs.at[i], dev(at, other))
 
     for p in (1, 2, 0):
         pass_on(p, 0)
@@ -316,8 +316,11 @@
             own = line[p].at[0, c]
             i = p * 8 + d * 2
             line_in[p, d * 2] = send(
-                own, line[p].at[4 - d, c], l_ss.at[i], l_rs.at[i], dev(along(p, d), c)
+                own, line[p].at[4 - d, c], l_ss.at[p * 2], l_rs.at[i], dev(along(p, d), c)
             )
+    for p in range(3):
+        drains.append((line[p].at[1:4, 0], l_ss.at[p * 2]))
+        drains.append((line[p].at[:, 0], l_ss.at[p * 2 + 1]))
 
     def pick(p, rel):
         line_in[p, (4 - rel) % 4 * 2 + 1].wait_recv()
@@ -347,37 +350,49 @@
             return ref.at[part, k]
         return ref.at[1:4, k]
 
+    def group(p, part):
+        return part if p == 0 else 2 + p * 2 + part
+
+    def step_of(p, part, k):
+        return part if p == 0 else (4 - k // 4) % 4
+
     def out(p, part, k):
-        j = part * 16 + k
         n = minus(k)
         return (
-            blocks(ds[p], p, part, k), rows(rr[p], p, part, n // 4, n % 4), d_ss.at[p * 64 + j],
-            d_rs.at[p * 64 + j], plane_dev(p, k),
+            blocks(ds[p], p, part, k), rows(rr[p], p, part, n // 4, n % 4), d_ss.at[group(p, part)],
+            d_rs.at[p * 4 + step_of(p, part, k)], plane_dev(p, k),
         )
 
     def back(p, part, k):
-        j = part * 16 + k
         return (
-            rows(oo[p], p, part, k // 4, k % 4), blocks(rt[p], p, part, minus(k)), e_ss.at[p * 64 + j],
-            e_rs.at[p * 64 + j], plane_dev(p, k),
-        )
-
-    d_in, e_in = {}, {}
+            rows(oo[p], p, part, k // 4, k % 4), blocks(rt[p], p, part, minus(k)), e_ss.at[group(p, part)],
+            e_rs.at[group(p, part)], plane_dev(p, k),
+        )
 
     def go(p, part, k):
-        d_in[p, part, k] = send(*out(p, part, k))
+        if k:
+            send(*out(p, part, k))
+        else:
+            src, dst, _, sem, _ = out(p, part, k)
+            keep(src, dst, sem)
+
+    def come(p, part, k):
+        if k:
+            send(*back(p, part, k))
+        else:
+            src, dst, _, sem, _ = back(p, part, k)
+            keep(src, dst, sem)
+
+    for p in range(3):
+        for part in range(4 if p == 0 else 2):
+            whole = ds[p].at[part, 1:16] if p == 0 or part == 0 else ds[p].at[1:4, 1:16]
+            drains.append((whole, d_ss.at[group(p, part)]))
+            drains.append((whole, e_ss.at[group(p, part)]))
 
     for p in (1, 2, 0):
         pick(p, 0)
-        for k in ORDER:
+        for k in (*ORDER, 0):
             go(p, 0, k)
-    for p in range(3):
-        if p == 0:
-            r0[0, 0, 0] = ds0[0, 0]
-        elif p == 1:
-            r1[0, 0, 0] = ds1[0, 0]
-        else:
-            r2[0, 0, 0] = ds2[0, 0]
     for d in (1, 3, 2):
         for p in (1, 2, 0):
             line_in[p, d * 2].wait_recv()
@@ -385,17 +400,14 @@
     for rel in (3, 1, 2):
         for p in (1, 2):
             pick(p, rel)
-    r1[0, 1:4, 0] = ds1[1:4, 0]
-    r2[0, 0, 1:4] = ds2[1:4, 0]
     for i in STEPS:
         if i:
             pick(0, i)
-            r0[i, 0, 0] = ds0[i, 0]
+            go(0, i, 0)
         for b in (2, 1, 3, 0):
             k = (4 - i) % 4 * 4 + b
-            if k:
-                go(1, 1, k)
-                go(2, 1, k)
+            go(1, 1, k)
+            go(2, 1, k)
             if i:
                 for k in ORDER[b * 4 : b * 4 + 4]:
                     go(0, i, k)
@@ -418,34 +430,22 @@
             result = jnp.dot(act, wd_s[:, OFF[p] : OFF[p] + COLS[p]], preferred_element_type=F32)
             oo[p][i] = result.astype(BF).reshape(4, 4, 16, COLS[p])
 
-    def come(p, part, k):
-        e_in[p, part, k] = send(*back(p, part, k))
-
     for i in STEPS:
-        for k in range(1, 16):
-            d_in[0, i, k].wait_recv()
-        for b in range(4):
-            k = (4 - i) % 4 * 4 + b
-            if k:
-                for p in (1, 2):
-                    d_in[p, 0, k].wait_recv()
-                    d_in[p, 1, k].wait_recv()
+        for p in range(3):
+            arrived(rr[p].at[i], d_rs.at[p * 4 + i])
         expert_rows(i)
-        rt0[i, 0] = o0[i, 0, 0]
+        come(0, i, 0)
         for b in (2, 1, 3, 0):
             k = i * 4 + b
-            if k:
-                come(1, 1, k)
-                come(2, 1, k)
+            come(1, 1, k)
+            come(2, 1, k)
             for k in ORDER[b * 4 : b * 4 + 4]:
                 come(0, i, k)
-    for k in ORDER:
+    for k in (*ORDER, 0):
         for p in (1, 2):
             come(p, 0, k)
-    rt1[:, 0] = o1[0, :, 0]
-    rt2[:, 0] = o2[0, 0]
-
-    x_in, p_in = {}, []
+
+    x_in = {}
 
     def combine(p, d):
         sums = jnp.dot(
@@ -454,7 +454,7 @@
         pf[p][d] = jnp.where(c == 0, sums[0], sums[1])
         px[p][d] = jnp.where(c == 0, sums[1], sums[0]).astype(BF)
         i = p * 4 + d
-        x_in[p, d] = send(px[p].at[d], xr[p].at[d], x_ss.at[i], x_rs.at[i], dev(at, other))
+        x_in[p, d] = send(px[p].at[d], xr[p].at[d], x_ss.at[p], x_rs.at[i], dev(at, other))
 
     def give(p, d):
         x_in[p, d].wait_recv()
@@ -463,43 +463,37 @@
             pf[p][d] = total
             return
         ps[p][d] = total.astype(BF)
-        i = p * 4 + d
-        p_in.append(send(ps[p].at[d], pr[p].at[d], p_ss.at[i], p_rs.at[i], dev(along(p, d), c)))
+        send(ps[p].at[d], pr[p].at[d], p_ss.at[p], p_rs.at[p], dev(along(p, d), c))
 
     for i in STEPS[:3]:
-        for k in range(1, 16):
-            e_in[0, i, k].wait_recv()
+        arrived(rt0.at[i], e_rs.at[group(0, i)])
         combine(0, i)
     for d in STEPS[:3]:
         give(0, d)
-    for k in range(1, 16):
-        for p in (1, 2):
-            e_in[p, 1, k].wait_recv()
+    for p in (1, 2):
+        arrived(rt[p].at[1:4], e_rs.at[group(p, 1)])
     for d in (2, 1, 3):
         for p in (1, 2):
             combine(p, d)
     for d in (2, 1, 3):
         for p in (1, 2):
             give(p, d)
-    for k in range(1, 16):
-        e_in[0, 0, k].wait_recv()
-    combine(0, 0)
-    for p in (1, 2):
-        for k in range(1, 16):
-            e_in[p, 0, k].wait_recv()
+    for p in range(3):
+        arrived(rt[p].at[0], e_rs.at[group(p, 0)])
         combine(p, 0)
+        drains.append((xr[p], x_ss.at[p]))
+        drains.append((pr[p].at[1:4], p_ss.at[p]))
     for p in range(3):
         give(p, 0)
-    for copy in p_in:
-        copy.wait_recv()
+        arrived(pr[p].at[1:4], p_rs.at[p])
     for p in range(3):
         columns = slice(OFF[p], OFF[p] + COLS[p])
         total = pj_s[:, columns] + pf[p][0]
         for d in range(1, 4):
             total = total + pr[p][d].astype(F32)
         out_ref[:, columns] = total
-    for copy in sent:
-        copy.wait_send()
+    for ref, sem in drains:
+        arrived(ref, sem)
 
 
 def layer(queries, key_rows, values, out_weight, expert_ids, gate_ints, w_gate, w_up, w_down):
@@ -519,9 +513,9 @@
         *by(4, 2, 64), *by(4, 16, 16), *by(4, 4, 4, 16), *by(4, 4, 4, 16), *by(4, 16, 16),
         *[vm((4, 64, n), F32) for n in COLS], *by(4, 64), *by(4, 64), *by(4, 64), *by(4, 64),
         vm((2048, 768), BF), vm((2048, 768), BF), vm((768, 2048), BF),
-        sem(8), sem(4), sem(4), sem(16), sem(16), sem(8), sem(8), sem(16), sem(16), sem(16), sem(16),
-        sem(24), sem(24), sem(24), sem(24), sem(192), sem(192), sem(192), sem(192),
-        sem(12), sem(12), sem(12), sem(12), sem(8), sem(8), sem(32), sem(32),
+        sem(8), sem(1), sem(1), sem(3), sem(2), sem(2), sem(8), sem(4), sem(4), sem(1), sem(4),
+        sem(6), sem(3), sem(6), sem(24), sem(8), sem(12), sem(8), sem(8),
+        sem(3), sem(12), sem(3), sem(3), sem(2), sem(8), sem(2), sem(8),
     ]
     hbm = pl.BlockSpec(memory_space=pl.ANY)
     vmem = pl.BlockSpec(memory_space=pltpu.VMEM)

time: 127 us -> 119 us (0.937)
  Pallas kernels: 125 us -> 117 us
    pallas_call x1, Pallas kernels: 125 us -> 117 us  [layer(): pl.pallas_call(body, out_shape=jax.ShapeDtypeStruct((64, 2048), F32), in_...]
where the time goes in v4:
time: 119 us; the launch traced here: 118 us
  Pallas kernels  117 us (98%)
  local copies, waits for them, and re-layouts  1.87 us (2%)
    pallas_call x1, Pallas kernels, layer(): pl.pallas_call(body, out_shape=jax.ShapeDtypeStruct((64, 2048), F32), in_...  117 us

profile of v4, /device:TPU:3, one launch (start us, length us, event | category | flops | bytes accessed | tf_op | source)
XLA Modules:
  0.0 118.4 jit_solution(12858872109449532843)
XLA Ops:
  0.0 116.5 %shard_map.91 = f32[64,2048]{1,0:T(8,128)} custom-call(f32[8,256,128]{2,1,0:T(8,128)} %bitcast.11, f32[8,256,128]{2,1,0:T(8,128)} %bitcast.12, f32[8,256,128]{2,1,0:T(8,128)} %bitcast.13, bf16[128,2048]{1,0:T(8,128)(2,1)} %w_h.1, s32[8,64]{1,0:T(8,128)} %bitcast.14, s32[8,64]{1,0:T(8,128)} %bitcast.15, bf16[2048,768]{1,0:T(8,128)(2,1)} %bitcast.8, ...), custom_call_target="tpu_custom_call" | custom-call | flops 12999999488 | bytes 14000000 | tf_op jit(solution)/shard_map/pallas_call | solution.py:522
  116.5 1.9 %copy.11 = f32[64,2048]{1,0:T(8,128)} copy(f32[64,2048]{1,0:T(8,128)} %shard_map.91) | data formatting | bytes 1048576

commit v5 on v4

--- a/solution.py
+++ b/solution.py
@@ -17,7 +17,7 @@
 CB = 4
 CBW = 512
 HALF = 1024
-STEPS = (1, 2, 3, 0)
+STEPS = (2, 1, 3, 0)
 CHUNK = 256
 
 
@@ -192,12 +192,13 @@
         scores = lax.dot_general(qb, kb, (((1,), (1,)), ((), ())), preferred_element_type=F32)
         scores = jnp.where(lower, scores, 0.0).astype(BF)
         o_s[i] = jnp.dot(scores, v_s[i].astype(BF), preferred_element_type=F32)
-    for d in (1, 3, 2):
-        for v in range(2):
-            q_in[v, d].wait_recv()
-            got = quarter(v, (at[lines[v]] - d + 4) % 4)
-            for e in (2, 1, 3):
-                send(got, got, z_ss.at[v], z_rs.at[v * 4 + d], dev(along(2, e), c))
+        if i == 3:
+            for d in (1, 3, 2):
+                for v in range(2):
+                    q_in[v, d].wait_recv()
+                    got = quarter(v, (at[lines[v]] - d + 4) % 4)
+                    for e in (2, 1, 3):
+                        send(got, got, z_ss.at[v], z_rs.at[v * 4 + d], dev(along(2, e), c))
     arrived(st_r.at[1:4], st_rs.at[0])
     earlier = jnp.zeros((128, 128), F32)
     for d in (1, 2, 3):
@@ -228,39 +229,6 @@
     drains.append((ar1.at[1:4], at_ss.at[1]))
     drains.append((ar0.at[0], at_ss.at[2]))
 
-    for p in range(3):
-        arrived(meta[p], m_rs.at[p])
-    row_r = lax.broadcasted_iota(jnp.int32, (256, 128), 0)
-    base = lax.broadcasted_iota(jnp.int32, (8, 128), 1) // 64 * 1024
-    first, second = row_r // 64, (row_r // 16) % 4
-    for p in range(3):
-        one, two = (first + at[PLANE[p][0]]) % 4, (second + at[PLANE[p][1]]) % 4
-        if p == 0:
-            expert = two * 32 + one * 8 + x * 2 + c
-        elif p == 1:
-            expert = two * 32 + y * 8 + one * 2 + c
-        else:
-            expert = z * 32 + two * 8 + one * 2 + c
-        wanted = (row_r // 8) % 2 * 1024 + expert * 8 + row_r % 8
-
-        def make(d, carry, p=p, wanted=wanted):
-            both = meta[p][d].astype(F32)
-            code = jnp.concatenate([both[0, :8, :64], both[1, :8, :64]], axis=1) * 8.0
-            code = code + jnp.concatenate([both[0, 8:, :64], both[1, 8:, :64]], axis=1)
-            code = code.astype(jnp.int32) + base
-            weight = jnp.concatenate([both[0, :8, 64:], both[1, :8, 64:]], axis=1)
-            sel = jnp.zeros((256, 128), F32)
-            com = jnp.zeros((256, 128), F32)
-            for k in range(8):
-                hit = code[k : k + 1] == wanted
-                sel = jnp.where(hit, 1.0, sel)
-                com = jnp.where(hit, weight[k : k + 1], com)
-            sel_s[p, d] = sel.astype(BF)
-            com_s[p, d] = com.T.astype(BF)
-            return carry
-
-        lax.fori_loop(0, 4, make, 0)
-
     for d in (1, 3, 2):
         for v in range(2):
             w_in[v, d].wait_recv()
@@ -289,6 +257,40 @@
                 dev(along(v, d), c),
             )
     drains.append((rs_r.at[:, 1:4], rs_ss.at[0]))
+
+    for p in range(3):
+        arrived(meta[p], m_rs.at[p])
+    row_r = lax.broadcasted_iota(jnp.int32, (256, 128), 0)
+    base = lax.broadcasted_iota(jnp.int32, (8, 128), 1) // 64 * 1024
+    first, second = row_r // 64, (row_r // 16) % 4
+    for p in range(3):
+        one, two = (first + at[PLANE[p][0]]) % 4, (second + at[PLANE[p][1]]) % 4
+        if p == 0:
+            expert = two * 32 + one * 8 + x * 2 + c
+        elif p == 1:
+            expert = two * 32 + y * 8 + one * 2 + c
+        else:
+            expert = z * 32 + two * 8 + one * 2 + c
+        wanted = (row_r // 8) % 2 * 1024 + expert * 8 + row_r % 8
+
+        def make(d, carry, p=p, wanted=wanted):
+            both = meta[p][d].astype(F32)
+            code = jnp.concatenate([both[0, :8, :64], both[1, :8, :64]], axis=1) * 8.0
+            code = code + jnp.concatenate([both[0, 8:, :64], both[1, 8:, :64]], axis=1)
+            code = code.astype(jnp.int32) + base
+            weight = jnp.concatenate([both[0, :8, 64:], both[1, :8, 64:]], axis=1)
+            sel = jnp.zeros((256, 128), F32)
+            com = jnp.zeros((256, 128), F32)
+            for k in range(8):
+                hit = code[k : k + 1] == wanted
+                sel = jnp.where(hit, 1.0, sel)
+                com = jnp.where(hit, weight[k : k + 1], com)
+            sel_s[p, d] = sel.astype(BF)
+            com_s[p, d] = com.T.astype(BF)
+            return carry
+
+        lax.fori_loop(0, 4, make, 0)
+
     square = jnp.zeros((64, 1), F32)
     for b in range(CB):
         v, low = b % 2, (b % 2) * HALF + (b // 2) * CBW
@@ -391,7 +393,8 @@
 
     for p in (1, 2, 0):
         pick(p, 0)
-        for k in (*ORDER, 0):
+    for k in (*ORDER, 0):
+        for p in (1, 2, 0):
             go(p, 0, k)
     for d in (1, 3, 2):
         for p in (1, 2, 0):

time: 119 us -> 113 us (0.950); the launches traced: 118 us -> 111 us
  Pallas kernels: 117 us -> 109 us
    pallas_call x1, Pallas kernels: 117 us -> 109 us  [layer(): pl.pallas_call(body, out_shape=jax.ShapeDtypeStruct((64, 2048), F32), in_...]
where the time goes in v5:
time: 113 us; the launch traced here: 111 us
  Pallas kernels  109 us (96%)
  local copies, waits for them, and re-layouts  1.87 us (2%)
    pallas_call x1, Pallas kernels, layer(): pl.pallas_call(body, out_shape=jax.ShapeDtypeStruct((64, 2048), F32), in_...  109 us

profile of v5, /device:TPU:3, one launch (start us, length us, event | category | flops | bytes accessed | tf_op | source)
XLA Modules:
  0.0 110.9 jit_solution(5459962272497715875)
XLA Ops:
  0.0 109.0 %shard_map.91 = f32[64,2048]{1,0:T(8,128)} custom-call(f32[8,256,128]{2,1,0:T(8,128)} %bitcast.11, f32[8,256,128]{2,1,0:T(8,128)} %bitcast.12, f32[8,256,128]{2,1,0:T(8,128)} %bitcast.13, bf16[128,2048]{1,0:T(8,128)(2,1)} %w_h.1, s32[8,64]{1,0:T(8,128)} %bitcast.14, s32[8,64]{1,0:T(8,128)} %bitcast.15, bf16[2048,768]{1,0:T(8,128)(2,1)} %bitcast.8, ...), custom_call_target="tpu_custom_call" | custom-call | flops 12999999488 | bytes 14000000 | tf_op jit(solution)/shard_map/pallas_call | solution.py:525
  109.0 1.9 %copy.11 = f32[64,2048]{1,0:T(8,128)} copy(f32[64,2048]{1,0:T(8,128)} %shard_map.91) | data formatting | bytes 1048576

commit v6 on v5

--- a/solution.py
+++ b/solution.py
@@ -192,7 +192,7 @@
         scores = lax.dot_general(qb, kb, (((1,), (1,)), ((), ())), preferred_element_type=F32)
         scores = jnp.where(lower, scores, 0.0).astype(BF)
         o_s[i] = jnp.dot(scores, v_s[i].astype(BF), preferred_element_type=F32)
-        if i == 3:
+        if i == 2:
             for d in (1, 3, 2):
                 for v in range(2):
                     q_in[v, d].wait_recv()
@@ -311,8 +311,6 @@
         i = p * 8 + d * 2 + 1
         line_in[p, d * 2 + 1] = send(block, block, l_ss.at[p * 2 + 1], l_rs.at[i], dev(at, other))
 
-    for p in (1, 2, 0):
-        pass_on(p, 0)
     for d in (2, 1, 3):
         for p in (1, 2, 0):
             own = line[p].at[0, c]
@@ -320,6 +318,8 @@
             line_in[p, d * 2] = send(
                 own, line[p].at[4 - d, c], l_ss.at[p * 2], l_rs.at[i], dev(along(p, d), c)
             )
+    for p in (1, 2, 0):
+        pass_on(p, 0)
     for p in range(3):
         drains.append((line[p].at[1:4, 0], l_ss.at[p * 2]))
         drains.append((line[p].at[:, 0], l_ss.at[p * 2 + 1]))

time: 113 us -> 113 us (level)
  no operation moved by 1% of the time
where the time goes in v6:
time: 113 us; the launch traced here: 112 us
  Pallas kernels  110 us (97%)
  local copies, waits for them, and re-layouts  1.87 us (2%)
    pallas_call x1, Pallas kernels, layer(): pl.pallas_call(body, out_shape=jax.ShapeDtypeStruct((64, 2048), F32), in_...  110 us

profile of v6, /device:TPU:3, one launch (start us, length us, event | category | flops | bytes accessed | tf_op | source)
XLA Modules:
  0.0 111.7 jit_solution(10423531881401473821)
XLA Ops:
  0.0 109.9 %shard_map.91 = f32[64,2048]{1,0:T(8,128)} custom-call(f32[8,256,128]{2,1,0:T(8,128)} %bitcast.11, f32[8,256,128]{2,1,0:T(8,128)} %bitcast.12, f32[8,256,128]{2,1,0:T(8,128)} %bitcast.13, bf16[128,2048]{1,0:T(8,128)(2,1)} %w_h.1, s32[8,64]{1,0:T(8,128)} %bitcast.14, s32[8,64]{1,0:T(8,128)} %bitcast.15, bf16[2048,768]{1,0:T(8,128)(2,1)} %bitcast.8, ...), custom_call_target="tpu_custom_call" | custom-call | flops 12999999488 | bytes 14000000 | tf_op jit(solution)/shard_map/pallas_call | solution.py:525
  109.9 1.9 %copy.11 = f32[64,2048]{1,0:T(8,128)} copy(f32[64,2048]{1,0:T(8,128)} %shard_map.91) | data formatting | bytes 1048576
